TPU v7x, 256 devices: a whole 4x4x8 slice. The times are simulated.
256 devices in a mesh: dp: 32 (over x_lo, z, core), section: 8 (over x_hi, y).
Axes of the slice: x: 4 (x_hi: 2, x_lo: 2; x = x_hi * 2 + x_lo), y: 4, z: 8, core: 2. Of those that a mesh axis runs over, the one named last changes fastest.
Arguments:
- mels: bfloat16 [24576, 128], P('dp'), may hold values from -6 to 6
- lengths: int32 [128], P('dp'), may hold values from 48 to 96, as said below
- sub_weight: bfloat16 [256, 1536], replicated, may hold values from -0.375 to 0.375
- block_weight: bfloat16 [8, 1536, 1536], P('section'), may hold values from -0.15625 to 0.15625
- conv_kernel: float32 [8, 31, 1536], P('section'), may hold values from -1 to 1
- norm_gain: float32 [8, 1536], P('section'), may hold values from 0.1 to 1.9
- cotangent: bfloat16 [12288, 1536], P('dp'), may hold values from -0.053955078 to 0.053955078
Outputs:
- weight_grad: bfloat16 [8, 1536, 1536], P('section')
- kernel_grad: float32 [8, 31, 1536], P('section')
- gain_grad: float32 [8, 1536], P('section')
Inputs may be any that keep to these rules, and one draw needn't show every extreme that they name: `lengths`: frames of an utterance at or beyond its length are padding.
All inputs are finite; a program needn't handle non-finite values.
Results may differ from a plain program's by a relative error of at most 0.035.
Values may be sent and summed in bfloat16 or wider, within the bound.
No kernel may reach another device: no remote copies, remote signals or barrier semaphores. Data moves between devices by JAX's collectives and lax.ppermute only.
A program may use at most 128 MiB of HBM per device.

v0:
```python
import functools
import jax
import jax.numpy as jnp
from jax import lax
from jax.experimental import pallas as pl
from jax.experimental.pallas import tpu as pltpu
from jax.sharding import PartitionSpec as P

FRAMES = 96
EPS = 1e-05
LANES = 128
PAD = 16
TAPS = 31
BLOCK = 256
VMEM = 16 * 2**20


def taps_sum(padded, taps, cols, reverse):
    total = None
    for low in range(8):
        shifted = padded[pl.ds(low, FRAMES + 24), :]
        for high in range(4):
            j = 8 * high + low - 1
            if 0 <= j < TAPS:
                row = TAPS - 1 - j if reverse else j
                term = taps[row : row + 1, cols] * shifted[8 * high : 8 * high + FRAMES]
                total = term if total is None else total + term
    return total


def lane_tile(tile):
    return pl.ds(pl.multiple_of(tile * LANES, LANES), LANES)


def lane_block(chunk):
    return pl.ds(pl.multiple_of(chunk * BLOCK, BLOCK), BLOCK)


def clear_rims(padded):
    rim = jnp.zeros((padded.shape[0], PAD, LANES), jnp.float32)
    padded[:, 0:PAD, :] = rim
    padded[:, PAD + FRAMES :, :] = rim


def frame_rows(length):
    rows = lax.broadcasted_iota(jnp.int32, (FRAMES, LANES), 0)
    return (rows < length).astype(jnp.float32)


def forward_kernel(tick, info, recv, subs, weight, taps, gain, *rest):
    out, conv_all, norm_all, inv_all, hid_all, block_in, padded, total = rest[-8:]
    section = info[0]
    slot = tick - section
    width = out.shape[1]
    tiles = width // LANES
    chunks = width // BLOCK
    zeros = jnp.zeros((FRAMES, LANES), jnp.float32)

    @pl.when((slot >= 0) & (slot < subs.shape[0]))
    def _():
        @pl.when(section == 0)
        def _():
            block_in[...] = subs[slot]

        @pl.when(section != 0)
        def _():
            block_in[...] = recv[...]

        clear_rims(padded)
        mask = frame_rows(info[1 + slot])

        def add_up(tile, sums):
            return sums + block_in[:, lane_tile(tile)].astype(jnp.float32)

        centre = jnp.sum(lax.fori_loop(0, tiles, add_up, zeros, unroll=4), axis=1, keepdims=True)
        centre = jnp.broadcast_to(centre * (1.0 / width), (FRAMES, LANES))

        def add_squares(tile, sums):
            gap = block_in[:, lane_tile(tile)].astype(jnp.float32) - centre
            return sums + gap * gap

        spread = jnp.sum(
            lax.fori_loop(0, tiles, add_squares, zeros, unroll=4), axis=1, keepdims=True
        )
        inv_std = jnp.broadcast_to(lax.rsqrt(spread * (1.0 / width) + EPS), (FRAMES, LANES))
        inv_all[slot] = inv_std
        total[...] = block_in[...].astype(jnp.float32)
        hid_all[slot, :, 0:BLOCK] = jnp.zeros((FRAMES, BLOCK), jnp.bfloat16)

        def project(chunk):
            cols = lane_block(chunk)
            total[...] += jnp.dot(
                hid_all[slot, :, cols], weight[cols, :], preferred_element_type=jnp.float32
            )

        def one_chunk(chunk, carry):
            project(jnp.maximum(chunk - 1, 0))
            for step in range(BLOCK // LANES):
                cols = lane_tile(chunk * (BLOCK // LANES) + step)
                normed = (block_in[:, cols].astype(jnp.float32) - centre) * inv_std
                norm_all[slot, :, cols] = normed
                padded[step, PAD : PAD + FRAMES, :] = normed * gain[:, cols] * mask
                conv = taps_sum(padded.at[step], taps, cols, False)
                conv_all[slot, :, cols] = conv
                hid_all[slot, :, cols] = (conv / (1.0 + jnp.exp(-conv))).astype(jnp.bfloat16)
            return carry

        lax.fori_loop(0, chunks, one_chunk, 0)
        project(chunks - 1)
        out[...] = total[...].astype(jnp.bfloat16)


def forward_call(tick, info, recv, subs, weight, taps, gain, stash):
    groups, _, width = subs.shape
    f32, bf16 = jnp.float32, jnp.bfloat16
    shapes = (
        jax.ShapeDtypeStruct((FRAMES, width), bf16),
        jax.ShapeDtypeStruct((groups, FRAMES, width), f32),
        jax.ShapeDtypeStruct((groups, FRAMES, width), f32),
        jax.ShapeDtypeStruct((groups, FRAMES, LANES), f32),
        jax.ShapeDtypeStruct((groups, FRAMES, width), bf16),
    )
    smem = pl.BlockSpec(memory_space=pltpu.SMEM)
    vmem = pl.BlockSpec(memory_space=pltpu.VMEM)
    held = () if stash is None else tuple(stash)
    res = pl.pallas_call(
        functools.partial(forward_kernel, tick),
        out_shape=shapes,
        in_specs=[smem] + [vmem] * (5 + len(held)),
        out_specs=(vmem,) * 5,
        scratch_shapes=[
            pltpu.VMEM((FRAMES, width), bf16),
            pltpu.VMEM((BLOCK // LANES, FRAMES + 2 * PAD, LANES), f32),
            pltpu.VMEM((FRAMES, width), f32),
        ],
        input_output_aliases={6 + i: 1 + i for i in range(len(held))},
        compiler_params=pltpu.CompilerParams(vmem_limit_bytes=VMEM),
        cost_estimate=pl.CostEstimate(
            flops=8 * FRAMES * width * width, bytes_accessed=width * width * 2, transcendentals=0
        ),
        name="section_forward",
    )(info, recv, subs, weight, taps, gain, *held)
    return res[0], res[1:]


def backward_kernel(tick, sections, info, recv, seeds, weight, taps, gain, conv_all, norm_all, inv_all, *rest):
    out, grad_all, gconv_all, gain_all = rest[-10:-6]
    grad_out, padded, scaled_now, ahead, mean_sum, dot_sum = rest[-6:]
    section = info[0]
    slot = tick - (sections - 1 - section)
    width = out.shape[1]
    tiles = width // LANES
    chunks = width // BLOCK

    @pl.when((slot >= 0) & (slot < seeds.shape[0]))
    def _():
        mask = frame_rows(info[1 + slot])

        @pl.when(section == sections - 1)
        def _():
            def seed(tile, carry):
                cols = lane_tile(tile)
                masked = seeds[slot, :, cols].astype(jnp.float32) * mask
                grad_out[:, cols] = masked.astype(jnp.bfloat16)
                return carry

            lax.fori_loop(0, tiles, seed, 0)

        @pl.when(section != sections - 1)
        def _():
            grad_out[...] = recv[...]

        clear_rims(padded)
        grad_all[slot] = grad_out[...]
        mean_sum[...] = jnp.zeros((FRAMES, LANES), jnp.float32)
        dot_sum[...] = jnp.zeros((FRAMES, LANES), jnp.float32)

        def back_project(chunk):
            return lax.dot_general(
                grad_out[...],
                weight[lane_block(chunk), :],
                (((1,), (1,)), ((), ())),
                preferred_element_type=jnp.float32,
            )

        ahead[0] = back_project(0)

        def one_chunk(chunk, carry):
            grad_hidden = ahead[chunk % 2]
            ahead[(chunk + 1) % 2] = back_project(jnp.minimum(chunk + 1, chunks - 1))
            for step in range(BLOCK // LANES):
                cols = lane_tile(chunk * (BLOCK // LANES) + step)
                conv = conv_all[slot, :, cols]
                sigma = 1.0 / (1.0 + jnp.exp(-conv))
                gconv = grad_hidden[:, step * LANES : (step + 1) * LANES] * sigma * (
                    1.0 + conv * (1.0 - sigma)
                )
                gconv_all[slot, :, cols] = gconv
                padded[step, PAD : PAD + FRAMES, :] = gconv
                grad_normed = taps_sum(padded.at[step], taps, cols, True) * mask
                normed = norm_all[slot, :, cols]
                product = grad_normed * normed
                part = product[0:8]
                for row in range(8, FRAMES, 8):
                    part = part + product[row : row + 8]
                gain_all[slot, :, cols] = part
                scaled = grad_normed * gain[:, cols]
                scaled_now[:, cols] = scaled
                mean_sum[...] += scaled
                dot_sum[...] += scaled * normed
            return carry

        lax.fori_loop(0, chunks, one_chunk, 0)
        mean_row = jnp.sum(mean_sum[...], axis=1, keepdims=True) * (1.0 / width)
        dot_row = jnp.sum(dot_sum[...], axis=1, keepdims=True) * (1.0 / width)
        mean_row = jnp.broadcast_to(mean_row, (FRAMES, LANES))
        dot_row = jnp.broadcast_to(dot_row, (FRAMES, LANES))
        inv_std = inv_all[slot]

        def finish(tile, carry):
            cols = lane_tile(tile)
            change = inv_std * (scaled_now[:, cols] - mean_row - norm_all[slot, :, cols] * dot_row)
            out[:, cols] = (grad_out[:, cols].astype(jnp.float32) + change).astype(jnp.bfloat16)
            return carry

        lax.fori_loop(0, tiles, finish, 0, unroll=2)


def backward_call(tick, sections, info, recv, seeds, weight, taps, gain, stash, held):
    groups, _, width = seeds.shape
    f32, bf16 = jnp.float32, jnp.bfloat16
    shapes = (
        jax.ShapeDtypeStruct((FRAMES, width), bf16),
        jax.ShapeDtypeStruct((groups, FRAMES, width), bf16),
        jax.ShapeDtypeStruct((groups, FRAMES, width), f32),
        jax.ShapeDtypeStruct((groups, 8, width), f32),
    )
    smem = pl.BlockSpec(memory_space=pltpu.SMEM)
    vmem = pl.BlockSpec(memory_space=pltpu.VMEM)
    held = () if held is None else tuple(held)
    res = pl.pallas_call(
        functools.partial(backward_kernel, tick, sections),
        out_shape=shapes,
        in_specs=[smem] + [vmem] * (8 + len(held)),
        out_specs=(vmem,) * 4,
        scratch_shapes=[
            pltpu.VMEM((FRAMES, width), bf16),
            pltpu.VMEM((BLOCK // LANES, FRAMES + 2 * PAD, LANES), f32),
            pltpu.VMEM((FRAMES, width), f32),
            pltpu.VMEM((2, FRAMES, BLOCK), f32),
            pltpu.VMEM((FRAMES, LANES), f32),
            pltpu.VMEM((FRAMES, LANES), f32),
        ],
        input_output_aliases={9 + i: 1 + i for i in range(len(held))},
        compiler_params=pltpu.CompilerParams(vmem_limit_bytes=VMEM),
        cost_estimate=pl.CostEstimate(
            flops=8 * FRAMES * width * width, bytes_accessed=width * width * 2, transcendentals=0
        ),
        name="section_backward",
    )(info, recv, seeds, weight, taps, gain, *stash[:3], *held)
    return res[0], res[1:]


def taps_kernel(tick, sections, info, gconv_all, norm_all, gain, gain_all, *rest):
    out, padded = rest[-2:]
    slot = tick - (sections - 1 - info[0])
    width = out.shape[1]
    if len(rest) == 2:
        out[...] = jnp.zeros(out.shape, jnp.float32)

    @pl.when((slot >= 0) & (slot < gconv_all.shape[0]))
    def _():
        mask = frame_rows(info[1 + slot])
        clear_rims(padded)

        def one_tile(tile, carry):
            cols = lane_tile(tile)
            padded[0, PAD : PAD + FRAMES, :] = norm_all[slot, :, cols] * gain[:, cols] * mask
            grads = gconv_all[slot, :, cols]
            for low in range(8):
                shifted = padded[0, pl.ds(low, FRAMES + 24), :]
                for high in range(4):
                    j = 8 * high + low - 1
                    if 0 <= j < TAPS:
                        product = grads * shifted[8 * high : 8 * high + FRAMES]
                        part = product[0:8]
                        for row in range(8, FRAMES, 8):
                            part = part + product[row : row + 8]
                        out[j : j + 1, cols] += jnp.sum(part, axis=0, keepdims=True)
            out[TAPS : TAPS + 1, cols] += jnp.sum(gain_all[slot, :, cols], axis=0, keepdims=True)
            return carry

        lax.fori_loop(0, width // LANES, one_tile, 0)


def on_chip(kernel, name, shapes, operands, scratch=(), aliases=None, flops=10**9, hbm_out=()):
    vmem = pl.BlockSpec(memory_space=pltpu.VMEM)
    smem = pl.BlockSpec(memory_space=pltpu.SMEM)
    anywhere = pl.BlockSpec(memory_space=pl.ANY)
    aliases = aliases or {}
    return pl.pallas_call(
        kernel,
        out_shape=tuple(jax.ShapeDtypeStruct(shape, dtype) for shape, dtype in shapes),
        in_specs=[smem]
        + [anywhere if aliases.get(i + 1) in hbm_out else vmem for i in range(len(operands) - 1)],
        out_specs=tuple(anywhere if i in hbm_out else vmem for i in range(len(shapes))),
        scratch_shapes=list(scratch),
        input_output_aliases=aliases,
        compiler_params=pltpu.CompilerParams(vmem_limit_bytes=VMEM),
        cost_estimate=pl.CostEstimate(flops=flops, bytes_accessed=2**20, transcendentals=0),
        name=name,
    )(*operands)


def taps_call(tick, sections, info, held, stash, gain, sums):
    width = gain.shape[1]
    operands = (info, held[1], stash[1], gain, held[2]) + (() if sums is None else (sums,))
    return on_chip(
        functools.partial(taps_kernel, tick, sections),
        "taps_gradient",
        [((TAPS + 1, width), jnp.float32)],
        operands,
        [pltpu.VMEM((1, FRAMES + 2 * PAD, LANES), jnp.float32)],
        {} if sums is None else {5: 0},
    )[0]


EXTRA = 8


def part_kernel(own, info, hid_all, grad_all, sums, out):
    ring, sides, rows, width = out.shape
    cut = rows - EXTRA
    half = info[5] if own else 1 - info[5]
    piece = 8 * cut
    tokens = hid_all.shape[0] * FRAMES
    grads = grad_all[...].reshape(tokens, width)
    for step in range(ring * sides * cut // piece):
        start = pl.multiple_of(half * (ring * sides * cut) + step * piece, LANES)
        hidden = hid_all[:, :, pl.ds(start, piece)].reshape(tokens, piece)
        part = lax.dot_general(
            hidden, grads, (((0,), (0,)), ((), ())), preferred_element_type=jnp.float32
        )
        for i in range(piece // cut):
            block = step * (piece // cut) + i
            out[block // sides, block % sides, 0:cut] = part[i * cut : (i + 1) * cut].astype(
                jnp.bfloat16
            )
    rest = jnp.zeros((EXTRA - 1, width), jnp.float32)
    for block in range(ring * sides):
        row = sums[pl.ds(half * (ring * sides) + block, 1), :]
        out[block // sides, block % sides, cut:] = jnp.concatenate([row, rest], axis=0).astype(
            jnp.bfloat16
        )


def merge_kernel(info, mine, other, own, *sends):
    ring = mine.shape[0]
    place, side = info[6], info[7]
    ahead, behind = ring // 2, ring - 1 - ring // 2

    def add(owner, x):
        owner = owner % ring
        return (mine[owner, x].astype(jnp.float32) + other[owner, x].astype(jnp.float32)).astype(
            jnp.bfloat16
        )

    for step, send in enumerate(sends):
        send[0] = add(place + ahead - step, 1 - side)
        send[1] = add(place + ring - behind + step, 1 - side)
    for owner in range(ring):
        own[owner] = add(owner, side)


def ring_kernel(step, info, own, crossed, *rest):
    ring = own.shape[0]
    place = info[6]
    ahead, behind = ring // 2, ring - 1 - ring // 2
    up = own[(place + ahead - step) % ring].astype(jnp.float32) + crossed[0].astype(jnp.float32)
    down = own[(place + ring - behind + step) % ring].astype(jnp.float32) + crossed[1].astype(
        jnp.float32
    )
    if len(rest) == 4:
        up = up + rest[0][...].astype(jnp.float32)
        down = down + rest[1][...].astype(jnp.float32)
    rest[-2][...] = up.astype(rest[-2].dtype)
    rest[-1][...] = down.astype(rest[-1].dtype)


def place_kernel(ring, sources, count, info, *rest):
    blocks = rest[:count]
    whole, edge, sems = rest[-3:]
    core, place, side = info[5], info[6], info[7]
    cut = blocks[0].shape[-2] - EXTRA
    copies = []
    for n, (which, i, offset, core_flip, side_flip) in enumerate(sources):
        block = blocks[which] if i is None else blocks[which].at[i]
        half = 1 - core if core_flip else core
        x = 1 - side if side_flip else side
        index = (half * ring + (place + offset + ring) % ring) * 2 + x
        start = pl.multiple_of(index * cut, cut)
        copy = pltpu.make_async_copy(
            block.at[pl.ds(0, cut)], whole.at[pl.ds(start, cut)], sems.at[n]
        )
        copy.start()
        copies.append(copy)
        edge[index] = block[cut:, :].astype(jnp.float32)
    for copy in copies:
        copy.wait()


def place_call(info, pieces, shape, ring, held):
    blocks, sources = [], []
    for block, i, offset, core_flip, side_flip in pieces:
        which = [n for n, other in enumerate(blocks) if other is block]
        if not which:
            which = [len(blocks)]
            blocks.append(block)
        sources.append((which[0], i, offset, core_flip, side_flip))
    count = len(blocks)
    return on_chip(
        functools.partial(place_kernel, ring, sources, count),
        "place_sums",
        [(shape, jnp.bfloat16), ((4 * ring, EXTRA, shape[1]), jnp.float32)],
        (info, *blocks, *(held or ())),
        [pltpu.SemaphoreType.DMA((len(sources),))],
        {count + 1: 0, count + 2: 1} if held else {},
        hbm_out=(0,),
    )


def column_sum(info, hidden, grads, sums, shards):
    ring = shards // 4
    width = grads.shape[2]
    cut = width // shards
    rows = cut + EXTRA
    f32, bf16 = jnp.float32, jnp.bfloat16

    def along_z(block, step):
        route = []
        for d in range(shards):
            x, z, c = d // (2 * ring), (d // 2) % ring, d % 2
            route.append((d, (x * ring + (z + step) % ring) * 2 + c))
        return lax.ppermute(block, "dp", route)

    def to_core(block):
        return lax.ppermute(block, "dp", [(d, d ^ 1) for d in range(shards)])

    def to_x(block):
        return lax.ppermute(block, "dp", [(d, (d + shards // 2) % shards) for d in range(shards)])

    def part(own):
        return on_chip(
            functools.partial(part_kernel, own),
            "weight_part",
            [((ring, 2, rows, width), bf16)],
            (info, hidden, grads, sums),
            flops=4 * 10**9,
        )[0]

    swapped = to_core(part(False))
    mine = part(True)
    ahead, behind = ring // 2, ring - 1 - ring // 2
    merged = on_chip(
        merge_kernel,
        "merge_cores",
        [((ring, rows, width), bf16)] + [((2, rows, width), bf16)] * ahead,
        (info, mine, swapped),
    )
    own, crossed = merged[0], [to_x(send) for send in merged[1:]]
    up = down = None
    for step in range(ahead):
        arrived = () if step == 0 else (up, down)
        last = step == ahead - 1
        up, down = on_chip(
            functools.partial(ring_kernel, step),
            "ring_step",
            [((rows, width), bf16), ((rows, width), f32 if last else bf16)],
            (info, own, crossed[step], *arrived),
        )
        up = along_z(up, 1)
        if not last:
            down = along_z(down, -1)
    done = (down + up.astype(f32)).astype(bf16)

    ups, downs = [done], [done]
    pieces = []

    def spread(blocks, offsets):
        stack = jnp.stack(blocks) if len(blocks) > 1 else blocks[0]
        index = range(len(blocks)) if len(blocks) > 1 else [None]
        crossed = to_x(stack)
        for array, core_flip, side_flip in (
            (stack, False, False),
            (crossed, False, True),
            (to_core(stack), True, False),
            (to_core(crossed), True, True),
        ):
            for i, offset in zip(index, offsets):
                pieces.append((array, i, offset, core_flip, side_flip))

    for step in range(1, ahead + 1):
        ups.append(along_z(ups[-1], 1))
        if step <= behind:
            downs.append(along_z(downs[-1], -1))
        if step == 1:
            spread([done, ups[1], downs[1]], [0, -1, 1])
        elif step <= behind:
            spread([ups[step], downs[step]], [-step, step])
            if step == behind - 1:
                early = place_call(info, pieces, (width, width), ring, None)
                pieces.clear()
        else:
            spread([ups[step]], [-step])
    whole, edge = place_call(info, pieces, (width, width), ring, early)
    edge = edge[:, 0]
    return whole, edge[:TAPS], edge[TAPS:]


def body(mels, lengths, sub_weight, block_weight, conv_kernel, norm_gain, cotangent):
    weight = block_weight[0]
    taps = conv_kernel[0]
    gain = norm_gain
    width = cotangent.shape[1]
    groups = lengths.shape[0]
    sections = lax.axis_size("section")
    shards = lax.axis_size("dp")
    section_idx = lax.axis_index("section")
    crossing = sections // 2

    def flip(shard):
        return (shard + shards // 2) % shards

    def linear(shard, section):
        return shard * sections + section

    def relay(block, pairs):
        route = []
        for source, target in pairs:
            crossed = (source < crossing) != (target < crossing)
            for shard in range(shards):
                there = flip(shard) if crossed else shard
                route.append((linear(shard, source), linear(there, target)))
        return lax.ppermute(block, ("dp", "section"), route)

    upper = range(crossing, sections)
    lens_flipped = lax.ppermute(
        lengths,
        ("dp", "section"),
        [(linear(d, s), linear(flip(d), s)) for d in range(shards) for s in upper],
    )
    lens = jnp.where(section_idx >= crossing, lens_flipped, lengths)
    seeds = lax.ppermute(
        cotangent,
        ("dp", "section"),
        [(linear(d, sections - 1), linear(flip(d), sections - 1)) for d in range(shards)],
    ).reshape(groups, FRAMES, width)
    subs = (
        jnp.dot(
            mels.reshape(groups * FRAMES, -1), sub_weight, preferred_element_type=jnp.float32
        )
        .astype(jnp.bfloat16)
        .reshape(groups, FRAMES, width)
    )
    shard = lax.axis_index("dp")
    spot = jnp.stack([shard % 2, (shard // 2) % (shards // 4), shard // (shards // 2)])
    info = jnp.concatenate([section_idx.reshape(1), lens, spot]).astype(jnp.int32)
    turn = sections - 1
    ticks = turn + groups
    stash = held = sums = None
    fwd_recv = {}
    bwd_recv = {}
    idle = jnp.zeros((FRAMES, width), jnp.bfloat16)
    for tick in range(turn + ticks):
        if tick < ticks:
            block, stash = forward_call(
                tick, info, fwd_recv.pop(tick - 1, idle), subs, weight, taps, gain, stash
            )
            pairs = [(s, s + 1) for s in range(sections - 1) if 0 <= tick - s < groups]
            if pairs:
                fwd_recv[tick] = relay(block, pairs)
        back = tick - turn
        if back >= 0:
            block, held = backward_call(
                back, sections, info, bwd_recv.pop(back - 1, idle), seeds, weight, taps, gain, stash, held
            )
            pairs = [
                (s, s - 1)
                for s in range(1, sections)
                if 0 <= back - (sections - 1 - s) < groups
            ]
            if pairs:
                bwd_recv[back] = relay(block, pairs)
            sums = taps_call(back, sections, info, held, stash, gain, sums)
    weight_sum, taps_sums, gain_sum = column_sum(info, stash[3], held[0], sums, shards)
    return (weight_sum[None], taps_sums[None], gain_sum)


def solution(mesh):
    return jax.shard_map(
        body,
        mesh=mesh,
        in_specs=(
            P("dp", None),
            P("dp"),
            P(),
            P("section", None, None),
            P("section", None, None),
            P("section", None),
            P("dp", None),
        ),
        out_specs=(P("section", None, None), P("section", None, None), P("section", None)),
        check_vma=False,
    )
```

profile of v0, /device:TPU:1, one launch (start us, length us, event | category | flops | bytes accessed | tf_op | source)
XLA Modules:
  0.0 363.8 jit_solution(10074758859131490892)
XLA Ops:
  1.5 1.0 reshape.22
  2.5 0.9 copy.94
  4.1 2.3 copy-done.1
  6.5 3.4 section_forward.11
  9.9 1.4 collective-permute-start.1
  11.3 3.6 collective-permute-done.1.recv
  15.0 3.4 section_forward.12
  18.4 3.8 %collective-permute-start.2 = (bf16[96,1536]{1,0:T(8,128)(2,1)S(1)}, bf16[96,1536]{1,0:T(8,128)(2,1)S(1)}, u32[]{:S(2)}, u32[]{:S(2)}) collective-permute-start(bf16[96,1536]{1,0:T(8,128)(2,1)S(1)} %get-tuple-element.122), channel_id=1, source_target_pairs={{0,1},{8,9},{16,17},{24,25},{32,33},{40,41},{48,49},{56,57},{64,65... | collective-permute-start | bytes 884744 | tf_op jit(solution)/shard_map/ppermute | solution.py:544
  22.2 3.6 collective-permute-done.2.recv
  25.9 3.4 section_forward.13
  29.3 3.8 %collective-permute-start.3 = (bf16[96,1536]{1,0:T(8,128)(2,1)S(1)}, bf16[96,1536]{1,0:T(8,128)(2,1)S(1)}, u32[]{:S(2)}, u32[]{:S(2)}) collective-permute-start(bf16[96,1536]{1,0:T(8,128)(2,1)S(1)} %get-tuple-element.127), channel_id=1, source_target_pairs={{0,1},{8,9},{16,17},{24,25},{32,33},{40,41},{48,49},{56,57},{64,65... | collective-permute-start | bytes 884744 | tf_op jit(solution)/shard_map/ppermute | solution.py:544
  33.1 3.6 collective-permute-done.3.recv
  36.8 3.4 section_forward.14
  40.2 3.8 %collective-permute-start.4 = (bf16[96,1536]{1,0:T(8,128)(2,1)S(1)}, bf16[96,1536]{1,0:T(8,128)(2,1)S(1)}, u32[]{:S(2)}, u32[]{:S(2)}) collective-permute-start(bf16[96,1536]{1,0:T(8,128)(2,1)S(1)} %get-tuple-element.132), channel_id=1, source_target_pairs={{0,1},{8,9},{16,17},{24,25},{32,33},{40,41},{48,49},{56,57},{64,65... | collective-permute-start | bytes 884744 | tf_op jit(solution)/shard_map/ppermute | solution.py:544
  44.0 3.6 collective-permute-done.4.recv
  61.7 1.3 section_forward.21
  69.0 1.3 collective-permute-start.18
  70.8 103.5 %collective-permute-done.18.recv = bf16[96,1536]{1,0:T(8,128)(2,1)S(1)} collective-permute-done((bf16[96,1536]{1,0:T(8,128)(2,1)S(1)}, bf16[96,1536]{1,0:T(8,128)(2,1)S(1)}, u32[]{:S(2)}, u32[]{:S(2)}) %collective-permute-start.18) | collective-permute-done | bytes 294944 | tf_op jit(solution)/shard_map/ppermute | solution.py:544
  174.3 4.9 %section_backward.18 = (bf16[96,1536]{1,0:T(8,128)(2,1)S(1)}, bf16[4,96,1536]{2,1,0:T(8,128)(2,1)S(1)}, f32[4,96,1536]{2,1,0:T(8,128)S(1)}, f32[4,8,1536]{2,1,0:T(8,128)S(1)}) custom-call(s32[8]{0:T(128)S(1)} %concatenate.3.info, bf16[96,1536]{1,0:T(8,128)(2,1)S(1)} %collective-permute-done.18.recv, ...), custom_call_target="tpu_custom_call", output_to_operand_aliasing={{1}: (9, {}), {2}: (10, {}), {3}: (11, {})} | custom-call | flops 1811939328 | bytes 4718592 | tf_op jit(solution)/shard_map/section_backward/pallas_call | solution.py:241
  179.3 1.3 collective-permute-start.19
  180.6 2.3 taps_gradient.18.rest_0_
  182.9 11.5 %collective-permute-done.19.recv = bf16[96,1536]{1,0:T(8,128)(2,1)S(1)} collective-permute-done((bf16[96,1536]{1,0:T(8,128)(2,1)S(1)}, bf16[96,1536]{1,0:T(8,128)(2,1)S(1)}, u32[]{:S(2)}, u32[]{:S(2)}) %collective-permute-start.19) | collective-permute-done | bytes 294944 | tf_op jit(solution)/shard_map/ppermute | solution.py:544
  194.4 4.9 %section_backward.19 = (bf16[96,1536]{1,0:T(8,128)(2,1)S(1)}, bf16[4,96,1536]{2,1,0:T(8,128)(2,1)S(1)}, f32[4,96,1536]{2,1,0:T(8,128)S(1)}, f32[4,8,1536]{2,1,0:T(8,128)S(1)}) custom-call(s32[8]{0:T(128)S(1)} %concatenate.3.info, bf16[96,1536]{1,0:T(8,128)(2,1)S(1)} %collective-permute-done.19.recv, ...), custom_call_target="tpu_custom_call", output_to_operand_aliasing={{1}: (9, {}), {2}: (10, {}), {3}: (11, {})} | custom-call | flops 1811939328 | bytes 4718592 | tf_op jit(solution)/shard_map/section_backward/pallas_call | solution.py:241
  199.3 1.3 collective-permute-start.20
  200.6 2.3 taps_gradient.19.rest_0_
  203.0 13.2 %collective-permute-done.20.recv = bf16[96,1536]{1,0:T(8,128)(2,1)S(1)} collective-permute-done((bf16[96,1536]{1,0:T(8,128)(2,1)S(1)}, bf16[96,1536]{1,0:T(8,128)(2,1)S(1)}, u32[]{:S(2)}, u32[]{:S(2)}) %collective-permute-start.20) | collective-permute-done | bytes 294944 | tf_op jit(solution)/shard_map/ppermute | solution.py:544
  216.2 4.9 %section_backward.20 = (bf16[96,1536]{1,0:T(8,128)(2,1)S(1)}, bf16[4,96,1536]{2,1,0:T(8,128)(2,1)S(1)}, f32[4,96,1536]{2,1,0:T(8,128)S(1)}, f32[4,8,1536]{2,1,0:T(8,128)S(1)}) custom-call(s32[8]{0:T(128)S(1)} %concatenate.3.info, bf16[96,1536]{1,0:T(8,128)(2,1)S(1)} %collective-permute-done.20.recv, ...), custom_call_target="tpu_custom_call", output_to_operand_aliasing={{1}: (9, {}), {2}: (10, {}), {3}: (11, {})} | custom-call | flops 1811939328 | bytes 4718592 | tf_op jit(solution)/shard_map/section_backward/pallas_call | solution.py:241
  221.1 1.3 collective-permute-start.21
  222.4 2.3 taps_gradient.20.rest_0_
  224.7 3.8 %collective-permute-done.21.recv = bf16[96,1536]{1,0:T(8,128)(2,1)S(1)} collective-permute-done((bf16[96,1536]{1,0:T(8,128)(2,1)S(1)}, bf16[96,1536]{1,0:T(8,128)(2,1)S(1)}, u32[]{:S(2)}, u32[]{:S(2)}) %collective-permute-start.21) | collective-permute-done | bytes 294944 | tf_op jit(solution)/shard_map/ppermute | solution.py:544
  228.6 5.7 %section_backward.21 = (bf16[96,1536]{1,0:T(8,128)(2,1)}, bf16[4,96,1536]{2,1,0:T(8,128)(2,1)S(1)}, f32[4,96,1536]{2,1,0:T(8,128)S(1)}, f32[4,8,1536]{2,1,0:T(8,128)S(1)}) custom-call(s32[8]{0:T(128)S(1)} %concatenate.3.info, bf16[96,1536]{1,0:T(8,128)(2,1)S(1)} %collective-permute-done.21.recv, ...), custom_call_target="tpu_custom_call", output_to_operand_aliasing={{1}: (9, {}), {2}: (10, {}), {3}: (11, {})} | custom-call | flops 1811939328 | bytes 4718592 | tf_op jit(solution)/shard_map/section_backward/pallas_call | solution.py:241
  234.2 2.3 taps_gradient.21.sums
  236.5 2.0 weight_part.3
  238.6 19.7 %collective-permute-start.22 = (bf16[8,2,56,1536]{3,2,1,0:T(8,128)(2,1)S(1)}, bf16[8,2,56,1536]{3,2,1,0:T(8,128)(2,1)S(1)}, u32[]{:S(2)}, u32[]{:S(2)}) collective-permute-start(bf16[8,2,56,1536]{3,2,1,0:T(8,128)(2,1)S(1)} %weight_part.3), channel_id=1, source_target_pairs={{0,8},{8,0},{16,24},{24,16},{32,40},{40,32},{48,56},{56,48},{64,72... | collective-permute-start | bytes 8257544 | tf_op jit(solution)/shard_map/ppermute | solution.py:447
  258.3 2.0 weight_part.2.mine
  260.4 2.7 collective-permute-done.22.other
  263.0 1.2 merge_cores.1
  264.2 9.0 %collective-permute-start.26 = (bf16[2,56,1536]{2,1,0:T(8,128)(2,1)S(1)}, bf16[2,56,1536]{2,1,0:T(8,128)(2,1)S(1)}, u32[]{:S(2)}, u32[]{:S(2)}) collective-permute-start(bf16[2,56,1536]{2,1,0:T(8,128)(2,1)S(1)} %get-tuple-element.218), channel_id=1, source_target_pairs={{0,128},{8,136},{16,144},{24,152},{32,160},{40,168},{48,176},{56,1... | collective-permute-start | bytes 1032200 | tf_op jit(solution)/shard_map/ppermute | solution.py:450
  273.2 1.5 collective-permute-start.25
  274.6 7.8 %collective-permute-done.26.crossed = bf16[2,56,1536]{2,1,0:T(8,128)(2,1)S(1)} collective-permute-done((bf16[2,56,1536]{2,1,0:T(8,128)(2,1)S(1)}, bf16[2,56,1536]{2,1,0:T(8,128)(2,1)S(1)}, u32[]{:S(2)}, u32[]{:S(2)}) %collective-permute-start.26) | collective-permute-done | bytes 344096 | tf_op jit(solution)/shard_map/ppermute | solution.py:450
  283.2 3.1 collective-permute-start.28
  286.6 3.2 collective-permute-done.25.crossed
  290.6 3.1 collective-permute-start.30
  294.1 2.7 collective-permute-done.24.crossed
  297.5 1.0 collective-permute-start.31
  298.5 2.6 collective-permute-start.32
  301.1 3.0 collective-permute-done.23.crossed
  305.6 5.6 %collective-permute-done.33 = bf16[56,1536]{1,0:T(8,128)(2,1)S(1)} collective-permute-done((bf16[56,1536]{1,0:T(8,128)(2,1)S(1)}, bf16[56,1536]{1,0:T(8,128)(2,1)S(1)}, u32[]{:S(2)}, u32[]{:S(2)}) %collective-permute-start.33) | collective-permute-done | bytes 172064 | tf_op jit(solution)/shard_map/ppermute | solution.py:444
  311.2 1.5 collective-permute-start.37
  312.8 2.8 collective-permute-done.37
  315.6 2.7 collective-permute-start.38
  318.3 7.0 %collective-permute-start.48 = (bf16[3,56,1536]{2,1,0:T(8,128)(2,1)S(1)}, bf16[3,56,1536]{2,1,0:T(8,128)(2,1)S(1)}, u32[]{:S(2)}, u32[]{:S(2)}) collective-permute-start(bf16[3,56,1536]{2,1,0:T(8,128)(2,1)S(1)} %pad_maximum_fusion.rest_0_), channel_id=1, source_target_pairs={{0,8},{8,0},{16,24},{24,16},{32,40},{40,32},{48,56},{56,48},{64,72... | collective-permute-start | bytes 1548296 | tf_op jit(solution)/shard_map/ppermute | solution.py:447
  325.3 1.6 collective-permute-start.39
  327.0 3.8 %collective-permute-start.51 = (bf16[2,56,1536]{2,1,0:T(8,128)(2,1)S(1)}, bf16[2,56,1536]{2,1,0:T(8,128)(2,1)S(1)}, u32[]{:S(2)}, u32[]{:S(2)}) collective-permute-start(bf16[2,56,1536]{2,1,0:T(8,128)(2,1)S(1)} %pad_maximum_fusion.2.rest_4_), channel_id=1, source_target_pairs={{0,8},{8,0},{16,24},{24,16},{32,40},{40,32},{48,56},{56,48},{64,72... | collective-permute-start | bytes 1032200 | tf_op jit(solution)/shard_map/ppermute | solution.py:447
  332.4 5.6 %collective-permute-done.43.rest_4_ = bf16[56,1536]{1,0:T(8,128)(2,1)S(1)} collective-permute-done((bf16[56,1536]{1,0:T(8,128)(2,1)S(1)}, bf16[56,1536]{1,0:T(8,128)(2,1)S(1)}, u32[]{:S(2)}, u32[]{:S(2)}) %collective-permute-start.43) | collective-permute-done | bytes 172064 | tf_op jit(solution)/shard_map/ppermute | solution.py:444
  338.0 1.7 collective-permute-start.40
  339.7 3.9 %collective-permute-start.49 = (bf16[3,56,1536]{2,1,0:T(8,128)(2,1)S(1)}, bf16[3,56,1536]{2,1,0:T(8,128)(2,1)S(1)}, u32[]{:S(2)}, u32[]{:S(2)}) collective-permute-start(bf16[3,56,1536]{2,1,0:T(8,128)(2,1)S(1)} %collective-permute-done.47.rest_1_), channel_id=1, source_target_pairs={{0,8},{8,0},{16,24},{24,16},{32,40},{40,32},{48,56},{56,48},{64,72... | collective-permute-start | bytes 1548296 | tf_op jit(solution)/shard_map/ppermute | solution.py:447
  343.6 2.4 collective-permute-done.50.rest_5_
  346.0 1.3 collective-permute-start.52
  347.5 5.9 %collective-permute-done.40.rest_1_ = bf16[2,56,1536]{2,1,0:T(8,128)(2,1)S(1)} collective-permute-done((bf16[2,56,1536]{2,1,0:T(8,128)(2,1)S(1)}, bf16[2,56,1536]{2,1,0:T(8,128)(2,1)S(1)}, u32[]{:S(2)}, u32[]{:S(2)}) %collective-permute-start.40) | collective-permute-done | bytes 344096 | tf_op jit(solution)/shard_map/ppermute | solution.py:450
  353.4 1.3 collective-permute-start.42
  354.7 2.3 collective-permute-done.44.rest_5_
  357.9 2.3 place_sums.2
  360.3 1.9 place_sums.3
  (108 shorter events, 30.2 us)
Async XLA Ops:
  0.6 2.8 copy-start
  0.6 3.3 copy-start.4
  0.7 3.5 copy-start.3
  0.7 3.3 collective-permute-start
  4.1 2.3 copy-start.1
  6.5 8.5 %copy-start.2 = (bf16[1,1536,1536]{2,1,0:T(8,128)(2,1)S(1)}, bf16[1,1536,1536]{2,1,0:T(8,128)(2,1)}, u32[]{:S(2)}) copy-start(bf16[1,1536,1536]{2,1,0:T(8,128)(2,1)} %param.10) | copy-start | bytes 14155780
  9.9 5.1 %collective-permute-start.1 = (bf16[96,1536]{1,0:T(8,128)(2,1)S(1)}, bf16[96,1536]{1,0:T(8,128)(2,1)S(1)}, u32[]{:S(2)}, u32[]{:S(2)}) collective-permute-start(bf16[96,1536]{1,0:T(8,128)(2,1)S(1)} %get-tuple-element.117), channel_id=1, source_target_pairs={{0,1},{8,9},{16,17},{24,25},{32,33},{40,41},{48,49},{56,57},{64,65... | collective-permute-start | bytes 884744 | tf_op jit(solution)/shard_map/ppermute | solution.py:544
  18.4 7.5 %collective-permute-start.2 = (bf16[96,1536]{1,0:T(8,128)(2,1)S(1)}, bf16[96,1536]{1,0:T(8,128)(2,1)S(1)}, u32[]{:S(2)}, u32[]{:S(2)}) collective-permute-start(bf16[96,1536]{1,0:T(8,128)(2,1)S(1)} %get-tuple-element.122), channel_id=1, source_target_pairs={{0,1},{8,9},{16,17},{24,25},{32,33},{40,41},{48,49},{56,57},{64,65... | collective-permute-start | bytes 884744 | tf_op jit(solution)/shard_map/ppermute | solution.py:544
  29.3 7.5 %collective-permute-start.3 = (bf16[96,1536]{1,0:T(8,128)(2,1)S(1)}, bf16[96,1536]{1,0:T(8,128)(2,1)S(1)}, u32[]{:S(2)}, u32[]{:S(2)}) collective-permute-start(bf16[96,1536]{1,0:T(8,128)(2,1)S(1)} %get-tuple-element.127), channel_id=1, source_target_pairs={{0,1},{8,9},{16,17},{24,25},{32,33},{40,41},{48,49},{56,57},{64,65... | collective-permute-start | bytes 884744 | tf_op jit(solution)/shard_map/ppermute | solution.py:544
  40.2 7.5 %collective-permute-start.4 = (bf16[96,1536]{1,0:T(8,128)(2,1)S(1)}, bf16[96,1536]{1,0:T(8,128)(2,1)S(1)}, u32[]{:S(2)}, u32[]{:S(2)}) collective-permute-start(bf16[96,1536]{1,0:T(8,128)(2,1)S(1)} %get-tuple-element.132), channel_id=1, source_target_pairs={{0,1},{8,9},{16,17},{24,25},{32,33},{40,41},{48,49},{56,57},{64,65... | collective-permute-start | bytes 884744 | tf_op jit(solution)/shard_map/ppermute | solution.py:544
  47.7 1.3 copy-start.5
  48.2 1.4 collective-permute-start.5
  48.9 4.5 %collective-permute-start.11 = (bf16[384,1536]{1,0:T(8,128)(2,1)S(1)}, bf16[384,1536]{1,0:T(8,128)(2,1)S(1)}, u32[]{:S(2)}, u32[]{:S(2)}) collective-permute-start(bf16[384,1536]{1,0:T(8,128)(2,1)S(1)} %copy-done.5), channel_id=1, source_target_pairs={{7,135},{15,143},{23,151},{31,159},{39,167},{47,175},{55,183},{63,... | collective-permute-start | bytes 3538952 | tf_op jit(solution)/shard_map/ppermute | solution.py:553
  50.2 0.7 collective-permute-start.6
  51.5 0.7 collective-permute-start.7
  52.8 2.5 collective-permute-start.8
  54.0 2.5 collective-permute-start.12
  55.8 2.5 collective-permute-start.9
  57.1 2.5 collective-permute-start.13
  58.9 2.8 collective-permute-start.10
  60.2 2.8 collective-permute-start.14
  63.5 1.2 collective-permute-start.15
  65.3 1.2 collective-permute-start.16
  67.2 1.2 collective-permute-start.17
  69.0 105.3 %collective-permute-start.18 = (bf16[96,1536]{1,0:T(8,128)(2,1)S(1)}, bf16[96,1536]{1,0:T(8,128)(2,1)S(1)}, u32[]{:S(2)}, u32[]{:S(2)}) collective-permute-start(bf16[96,1536]{1,0:T(8,128)(2,1)S(1)} %get-tuple-element.195), channel_id=1, source_target_pairs={{1,0},{9,8},{17,16},{25,24},{33,32},{41,40},{49,48},{57,56},{65,64... | collective-permute-start | bytes 884744 | tf_op jit(solution)/shard_map/ppermute | solution.py:544
  179.3 15.2 %collective-permute-start.19 = (bf16[96,1536]{1,0:T(8,128)(2,1)S(1)}, bf16[96,1536]{1,0:T(8,128)(2,1)S(1)}, u32[]{:S(2)}, u32[]{:S(2)}) collective-permute-start(bf16[96,1536]{1,0:T(8,128)(2,1)S(1)} %get-tuple-element.199), channel_id=1, source_target_pairs={{1,0},{9,8},{17,16},{25,24},{33,32},{41,40},{49,48},{57,56},{65,64... | collective-permute-start | bytes 884744 | tf_op jit(solution)/shard_map/ppermute | solution.py:544
  199.3 16.8 %collective-permute-start.20 = (bf16[96,1536]{1,0:T(8,128)(2,1)S(1)}, bf16[96,1536]{1,0:T(8,128)(2,1)S(1)}, u32[]{:S(2)}, u32[]{:S(2)}) collective-permute-start(bf16[96,1536]{1,0:T(8,128)(2,1)S(1)} %get-tuple-element.203), channel_id=1, source_target_pairs={{1,0},{9,8},{17,16},{25,24},{33,32},{41,40},{49,48},{57,56},{65,64... | collective-permute-start | bytes 884744 | tf_op jit(solution)/shard_map/ppermute | solution.py:544
  221.1 7.5 %collective-permute-start.21 = (bf16[96,1536]{1,0:T(8,128)(2,1)S(1)}, bf16[96,1536]{1,0:T(8,128)(2,1)S(1)}, u32[]{:S(2)}, u32[]{:S(2)}) collective-permute-start(bf16[96,1536]{1,0:T(8,128)(2,1)S(1)} %get-tuple-element.207), channel_id=1, source_target_pairs={{1,0},{9,8},{17,16},{25,24},{33,32},{41,40},{49,48},{57,56},{65,64... | collective-permute-start | bytes 884744 | tf_op jit(solution)/shard_map/ppermute | solution.py:544
  238.6 24.5 %collective-permute-start.22 = (bf16[8,2,56,1536]{3,2,1,0:T(8,128)(2,1)S(1)}, bf16[8,2,56,1536]{3,2,1,0:T(8,128)(2,1)S(1)}, u32[]{:S(2)}, u32[]{:S(2)}) collective-permute-start(bf16[8,2,56,1536]{3,2,1,0:T(8,128)(2,1)S(1)} %weight_part.3), channel_id=1, source_target_pairs={{0,8},{8,0},{16,24},{24,16},{32,40},{40,32},{48,56},{56,48},{64,72... | collective-permute-start | bytes 8257544 | tf_op jit(solution)/shard_map/ppermute | solution.py:447
  264.2 18.2 %collective-permute-start.26 = (bf16[2,56,1536]{2,1,0:T(8,128)(2,1)S(1)}, bf16[2,56,1536]{2,1,0:T(8,128)(2,1)S(1)}, u32[]{:S(2)}, u32[]{:S(2)}) collective-permute-start(bf16[2,56,1536]{2,1,0:T(8,128)(2,1)S(1)} %get-tuple-element.218), channel_id=1, source_target_pairs={{0,128},{8,136},{16,144},{24,152},{32,160},{40,168},{48,176},{56,1... | collective-permute-start | bytes 1032200 | tf_op jit(solution)/shard_map/ppermute | solution.py:450
  273.2 16.6 %collective-permute-start.25 = (bf16[2,56,1536]{2,1,0:T(8,128)(2,1)S(1)}, bf16[2,56,1536]{2,1,0:T(8,128)(2,1)S(1)}, u32[]{:S(2)}, u32[]{:S(2)}) collective-permute-start(bf16[2,56,1536]{2,1,0:T(8,128)(2,1)S(1)} %get-tuple-element.217), channel_id=1, source_target_pairs={{0,128},{8,136},{16,144},{24,152},{32,160},{40,168},{48,176},{56,1... | collective-permute-start | bytes 1032200 | tf_op jit(solution)/shard_map/ppermute | solution.py:450
  283.1 6.7 %collective-permute-start.27 = (bf16[56,1536]{1,0:T(8,128)(2,1)S(1)}, bf16[56,1536]{1,0:T(8,128)(2,1)S(1)}, u32[]{:S(2)}, u32[]{:S(2)}) collective-permute-start(bf16[56,1536]{1,0:T(8,128)(2,1)S(1)} %get-tuple-element.219), channel_id=1, source_target_pairs={{0,16},{8,24},{16,32},{24,40},{32,48},{40,56},{48,64},{56,72},{64,... | collective-permute-start | bytes 516104 | tf_op jit(solution)/shard_map/ppermute | solution.py:444
  283.2 6.6 %collective-permute-start.28 = (bf16[56,1536]{1,0:T(8,128)(2,1)S(1)}, bf16[56,1536]{1,0:T(8,128)(2,1)S(1)}, u32[]{:S(2)}, u32[]{:S(2)}) collective-permute-start(bf16[56,1536]{1,0:T(8,128)(2,1)S(1)} %get-tuple-element.220), channel_id=1, source_target_pairs={{0,112},{8,120},{16,0},{24,8},{32,16},{40,24},{48,32},{56,40},{64,... | collective-permute-start | bytes 516104 | tf_op jit(solution)/shard_map/ppermute | solution.py:444
  286.3 10.5 %collective-permute-start.24 = (bf16[2,56,1536]{2,1,0:T(8,128)(2,1)S(1)}, bf16[2,56,1536]{2,1,0:T(8,128)(2,1)S(1)}, u32[]{:S(2)}, u32[]{:S(2)}) collective-permute-start(bf16[2,56,1536]{2,1,0:T(8,128)(2,1)S(1)} %get-tuple-element.216), channel_id=1, source_target_pairs={{0,128},{8,136},{16,144},{24,152},{32,160},{40,168},{48,176},{56,1... | collective-permute-start | bytes 1032200 | tf_op jit(solution)/shard_map/ppermute | solution.py:450
  290.5 6.3 %collective-permute-start.29 = (bf16[56,1536]{1,0:T(8,128)(2,1)S(1)}, bf16[56,1536]{1,0:T(8,128)(2,1)S(1)}, u32[]{:S(2)}, u32[]{:S(2)}) collective-permute-start(bf16[56,1536]{1,0:T(8,128)(2,1)S(1)} %get-tuple-element.221), channel_id=1, source_target_pairs={{0,16},{8,24},{16,32},{24,40},{32,48},{40,56},{48,64},{56,72},{64,... | collective-permute-start | bytes 516104 | tf_op jit(solution)/shard_map/ppermute | solution.py:444
  290.6 6.2 %collective-permute-start.30 = (bf16[56,1536]{1,0:T(8,128)(2,1)S(1)}, bf16[56,1536]{1,0:T(8,128)(2,1)S(1)}, u32[]{:S(2)}, u32[]{:S(2)}) collective-permute-start(bf16[56,1536]{1,0:T(8,128)(2,1)S(1)} %get-tuple-element.222), channel_id=1, source_target_pairs={{0,112},{8,120},{16,0},{24,8},{32,16},{40,24},{48,32},{56,40},{64,... | collective-permute-start | bytes 516104 | tf_op jit(solution)/shard_map/ppermute | solution.py:444
  293.7 10.3 %collective-permute-start.23 = (bf16[2,56,1536]{2,1,0:T(8,128)(2,1)S(1)}, bf16[2,56,1536]{2,1,0:T(8,128)(2,1)S(1)}, u32[]{:S(2)}, u32[]{:S(2)}) collective-permute-start(bf16[2,56,1536]{2,1,0:T(8,128)(2,1)S(1)} %get-tuple-element.215), channel_id=1, source_target_pairs={{0,128},{8,136},{16,144},{24,152},{32,160},{40,168},{48,176},{56,1... | collective-permute-start | bytes 1032200 | tf_op jit(solution)/shard_map/ppermute | solution.py:450
  297.5 6.6 %collective-permute-start.31 = (bf16[56,1536]{1,0:T(8,128)(2,1)S(1)}, bf16[56,1536]{1,0:T(8,128)(2,1)S(1)}, u32[]{:S(2)}, u32[]{:S(2)}) collective-permute-start(bf16[56,1536]{1,0:T(8,128)(2,1)S(1)} %get-tuple-element.223), channel_id=1, source_target_pairs={{0,16},{8,24},{16,32},{24,40},{32,48},{40,56},{48,64},{56,72},{64,... | collective-permute-start | bytes 516104 | tf_op jit(solution)/shard_map/ppermute | solution.py:444
  298.5 5.6 %collective-permute-start.32 = (bf16[56,1536]{1,0:T(8,128)(2,1)S(1)}, bf16[56,1536]{1,0:T(8,128)(2,1)S(1)}, u32[]{:S(2)}, u32[]{:S(2)}) collective-permute-start(bf16[56,1536]{1,0:T(8,128)(2,1)S(1)} %get-tuple-element.224), channel_id=1, source_target_pairs={{0,112},{8,120},{16,0},{24,8},{32,16},{40,24},{48,32},{56,40},{64,... | collective-permute-start | bytes 516104 | tf_op jit(solution)/shard_map/ppermute | solution.py:444
  304.8 6.4 %collective-permute-start.33 = (bf16[56,1536]{1,0:T(8,128)(2,1)S(1)}, bf16[56,1536]{1,0:T(8,128)(2,1)S(1)}, u32[]{:S(2)}, u32[]{:S(2)}) collective-permute-start(bf16[56,1536]{1,0:T(8,128)(2,1)S(1)} %get-tuple-element.226), channel_id=1, source_target_pairs={{0,16},{8,24},{16,32},{24,40},{32,48},{40,56},{48,64},{56,72},{64,... | collective-permute-start | bytes 516104 | tf_op jit(solution)/shard_map/ppermute | solution.py:444
  311.2 4.3 %collective-permute-start.37 = (bf16[56,1536]{1,0:T(8,128)(2,1)S(1)}, bf16[56,1536]{1,0:T(8,128)(2,1)S(1)}, u32[]{:S(2)}, u32[]{:S(2)}) collective-permute-start(bf16[56,1536]{1,0:T(8,128)(2,1)S(1)} %add_convert_fusion), channel_id=1, source_target_pairs={{0,112},{8,120},{16,0},{24,8},{32,16},{40,24},{48,32},{56,40},{64,... | collective-permute-start | bytes 516104 | tf_op jit(solution)/shard_map/ppermute | solution.py:444
  312.8 5.5 %collective-permute-start.34 = (bf16[56,1536]{1,0:T(8,128)(2,1)S(1)}, bf16[56,1536]{1,0:T(8,128)(2,1)S(1)}, u32[]{:S(2)}, u32[]{:S(2)}) collective-permute-start(bf16[56,1536]{1,0:T(8,128)(2,1)S(1)} %add_convert_fusion), channel_id=1, source_target_pairs={{0,16},{8,24},{16,32},{24,40},{32,48},{40,56},{48,64},{56,72},{64,... | collective-permute-start | bytes 516104 | tf_op jit(solution)/shard_map/ppermute | solution.py:444
  315.6 9.8 %collective-permute-start.38 = (bf16[56,1536]{1,0:T(8,128)(2,1)S(1)}, bf16[56,1536]{1,0:T(8,128)(2,1)S(1)}, u32[]{:S(2)}, u32[]{:S(2)}) collective-permute-start(bf16[56,1536]{1,0:T(8,128)(2,1)S(1)} %collective-permute-done.37), channel_id=1, source_target_pairs={{0,112},{8,120},{16,0},{24,8},{32,16},{40,24},{48,32},{56,40},{64,... | collective-permute-start | bytes 516104 | tf_op jit(solution)/shard_map/ppermute | solution.py:444
  318.2 8.7 %collective-permute-start.35 = (bf16[56,1536]{1,0:T(8,128)(2,1)S(1)}, bf16[56,1536]{1,0:T(8,128)(2,1)S(1)}, u32[]{:S(2)}, u32[]{:S(2)}) collective-permute-start(bf16[56,1536]{1,0:T(8,128)(2,1)S(1)} %collective-permute-done.34), channel_id=1, source_target_pairs={{0,16},{8,24},{16,32},{24,40},{32,48},{40,56},{48,64},{56,72},{64,... | collective-permute-start | bytes 516104 | tf_op jit(solution)/shard_map/ppermute | solution.py:444
  318.3 29.1 %collective-permute-start.48 = (bf16[3,56,1536]{2,1,0:T(8,128)(2,1)S(1)}, bf16[3,56,1536]{2,1,0:T(8,128)(2,1)S(1)}, u32[]{:S(2)}, u32[]{:S(2)}) collective-permute-start(bf16[3,56,1536]{2,1,0:T(8,128)(2,1)S(1)} %pad_maximum_fusion.rest_0_), channel_id=1, source_target_pairs={{0,8},{8,0},{16,24},{24,16},{32,40},{40,32},{48,56},{56,48},{64,72... | collective-permute-start | bytes 1548296 | tf_op jit(solution)/shard_map/ppermute | solution.py:447
  325.3 14.4 %collective-permute-start.47 = (bf16[3,56,1536]{2,1,0:T(8,128)(2,1)S(1)}, bf16[3,56,1536]{2,1,0:T(8,128)(2,1)S(1)}, u32[]{:S(2)}, u32[]{:S(2)}) collective-permute-start(bf16[3,56,1536]{2,1,0:T(8,128)(2,1)S(1)} %pad_maximum_fusion.rest_0_), channel_id=1, source_target_pairs={{0,128},{8,136},{16,144},{24,152},{32,160},{40,168},{48,176},{56,1... | collective-permute-start | bytes 1548296 | tf_op jit(solution)/shard_map/ppermute | solution.py:450
  325.3 5.5 %collective-permute-start.39 = (bf16[56,1536]{1,0:T(8,128)(2,1)S(1)}, bf16[56,1536]{1,0:T(8,128)(2,1)S(1)}, u32[]{:S(2)}, u32[]{:S(2)}) collective-permute-start(bf16[56,1536]{1,0:T(8,128)(2,1)S(1)} %collective-permute-done.38), channel_id=1, source_target_pairs={{0,112},{8,120},{16,0},{24,8},{32,16},{40,24},{48,32},{56,40},{64,... | collective-permute-start | bytes 516104 | tf_op jit(solution)/shard_map/ppermute | solution.py:444
  326.9 5.5 %collective-permute-start.36 = (bf16[56,1536]{1,0:T(8,128)(2,1)S(1)}, bf16[56,1536]{1,0:T(8,128)(2,1)S(1)}, u32[]{:S(2)}, u32[]{:S(2)}) collective-permute-start(bf16[56,1536]{1,0:T(8,128)(2,1)S(1)} %collective-permute-done.35), channel_id=1, source_target_pairs={{0,16},{8,24},{16,32},{24,40},{32,48},{40,56},{48,64},{56,72},{64,... | collective-permute-start | bytes 516104 | tf_op jit(solution)/shard_map/ppermute | solution.py:444
  327.0 20.3 %collective-permute-start.51 = (bf16[2,56,1536]{2,1,0:T(8,128)(2,1)S(1)}, bf16[2,56,1536]{2,1,0:T(8,128)(2,1)S(1)}, u32[]{:S(2)}, u32[]{:S(2)}) collective-permute-start(bf16[2,56,1536]{2,1,0:T(8,128)(2,1)S(1)} %pad_maximum_fusion.2.rest_4_), channel_id=1, source_target_pairs={{0,8},{8,0},{16,24},{24,16},{32,40},{40,32},{48,56},{56,48},{64,72... | collective-permute-start | bytes 1032200 | tf_op jit(solution)/shard_map/ppermute | solution.py:447
  330.8 15.2 %collective-permute-start.50 = (bf16[2,56,1536]{2,1,0:T(8,128)(2,1)S(1)}, bf16[2,56,1536]{2,1,0:T(8,128)(2,1)S(1)}, u32[]{:S(2)}, u32[]{:S(2)}) collective-permute-start(bf16[2,56,1536]{2,1,0:T(8,128)(2,1)S(1)} %pad_maximum_fusion.2.rest_4_), channel_id=1, source_target_pairs={{0,128},{8,136},{16,144},{24,152},{32,160},{40,168},{48,176},{56,1... | collective-permute-start | bytes 1032200 | tf_op jit(solution)/shard_map/ppermute | solution.py:450
  332.4 5.6 %collective-permute-start.43 = (bf16[56,1536]{1,0:T(8,128)(2,1)S(1)}, bf16[56,1536]{1,0:T(8,128)(2,1)S(1)}, u32[]{:S(2)}, u32[]{:S(2)}) collective-permute-start(bf16[56,1536]{1,0:T(8,128)(2,1)S(1)} %collective-permute-done.36), channel_id=1, source_target_pairs={{0,16},{8,24},{16,32},{24,40},{32,48},{40,56},{48,64},{56,72},{64,... | collective-permute-start | bytes 516104 | tf_op jit(solution)/shard_map/ppermute | solution.py:444
  338.0 15.4 %collective-permute-start.40 = (bf16[2,56,1536]{2,1,0:T(8,128)(2,1)S(1)}, bf16[2,56,1536]{2,1,0:T(8,128)(2,1)S(1)}, u32[]{:S(2)}, u32[]{:S(2)}) collective-permute-start(bf16[2,56,1536]{2,1,0:T(8,128)(2,1)S(1)} %pad_maximum_fusion.1.rest_0_), channel_id=1, source_target_pairs={{0,128},{8,136},{16,144},{24,152},{32,160},{40,168},{48,176},{56,1... | collective-permute-start | bytes 1032200 | tf_op jit(solution)/shard_map/ppermute | solution.py:450
  339.7 18.2 %collective-permute-start.49 = (bf16[3,56,1536]{2,1,0:T(8,128)(2,1)S(1)}, bf16[3,56,1536]{2,1,0:T(8,128)(2,1)S(1)}, u32[]{:S(2)}, u32[]{:S(2)}) collective-permute-start(bf16[3,56,1536]{2,1,0:T(8,128)(2,1)S(1)} %collective-permute-done.47.rest_1_), channel_id=1, source_target_pairs={{0,8},{8,0},{16,24},{24,16},{32,40},{40,32},{48,56},{56,48},{64,72... | collective-permute-start | bytes 1548296 | tf_op jit(solution)/shard_map/ppermute | solution.py:447
  346.0 11.9 %collective-permute-start.52 = (bf16[2,56,1536]{2,1,0:T(8,128)(2,1)S(1)}, bf16[2,56,1536]{2,1,0:T(8,128)(2,1)S(1)}, u32[]{:S(2)}, u32[]{:S(2)}) collective-permute-start(bf16[2,56,1536]{2,1,0:T(8,128)(2,1)S(1)} %collective-permute-done.50.rest_5_), channel_id=1, source_target_pairs={{0,8},{8,0},{16,24},{24,16},{32,40},{40,32},{48,56},{56,48},{64,72... | collective-permute-start | bytes 1032200 | tf_op jit(solution)/shard_map/ppermute | solution.py:447
  347.3 9.7 %collective-permute-start.44 = (bf16[56,1536]{1,0:T(8,128)(2,1)S(1)}, bf16[56,1536]{1,0:T(8,128)(2,1)S(1)}, u32[]{:S(2)}, u32[]{:S(2)}) collective-permute-start(bf16[56,1536]{1,0:T(8,128)(2,1)S(1)} %collective-permute-done.43.rest_4_), channel_id=1, source_target_pairs={{0,128},{8,136},{16,144},{24,152},{32,160},{40,168},{48,176},{56,1... | collective-permute-start | bytes 516104 | tf_op jit(solution)/shard_map/ppermute | solution.py:450
  347.4 12.9 %collective-permute-start.41 = (bf16[2,56,1536]{2,1,0:T(8,128)(2,1)S(1)}, bf16[2,56,1536]{2,1,0:T(8,128)(2,1)S(1)}, u32[]{:S(2)}, u32[]{:S(2)}) collective-permute-start(bf16[2,56,1536]{2,1,0:T(8,128)(2,1)S(1)} %pad_maximum_fusion.1.rest_0_), channel_id=1, source_target_pairs={{0,8},{8,0},{16,24},{24,16},{32,40},{40,32},{48,56},{56,48},{64,72... | collective-permute-start | bytes 1032200 | tf_op jit(solution)/shard_map/ppermute | solution.py:447
  353.4 6.9 %collective-permute-start.42 = (bf16[2,56,1536]{2,1,0:T(8,128)(2,1)S(1)}, bf16[2,56,1536]{2,1,0:T(8,128)(2,1)S(1)}, u32[]{:S(2)}, u32[]{:S(2)}) collective-permute-start(bf16[2,56,1536]{2,1,0:T(8,128)(2,1)S(1)} %collective-permute-done.40.rest_1_), channel_id=1, source_target_pairs={{0,8},{8,0},{16,24},{24,16},{32,40},{40,32},{48,56},{56,48},{64,72... | collective-permute-start | bytes 1032200 | tf_op jit(solution)/shard_map/ppermute | solution.py:447
  357.1 3.2 collective-permute-start.45
  357.9 2.4 collective-permute-start.46
where the time goes:
time: 368 us; the launch traced here: 364 us
  waiting for transfers between devices  191 us (52%)
  starting transfers between devices  96.1 us (26%)
  Pallas kernels  68.1 us (19%)
  local copies, waits for them, and re-layouts  5.8 us (2%)
    ppermute x20, waiting for transfers between devices, relay(): return lax.ppermute(block, ('dp', 'section'), route)  147 us
    ppermute x9, starting transfers between devices, to_core(): return lax.ppermute(block, 'dp', [(d, d ^ 1) for d in range(shards)])  38.1 us
    ppermute x8, waiting for transfers between devices, to_x(): lax.ppermute(block, 'dp', [(d, (d + shards // 2) % shards) for d in range...  27.4 us
    ppermute x20, starting transfers between devices, relay(): return lax.ppermute(block, ('dp', 'section'), route)  26.2 us
    pallas_call x20, Pallas kernels, on_chip(): pl.pallas_call(kernel, out_shape=tuple((jax.ShapeDtypeStruct(shape, dtype...  25.5 us
    pallas_call x11, Pallas kernels, backward_call(): pl.pallas_call(functools.partial(backward_kernel, tick, sections), out_sh...  24.3 us
    pallas_call x11, Pallas kernels, forward_call(): pl.pallas_call(functools.partial(forward_kernel, tick), out_shape=shapes,...  18.3 us
    ppermute x14, starting transfers between devices, along_z(): return lax.ppermute(block, 'dp', route)  16.8 us
  transfers between devices with their start and end apart: 53, of which 20 were waited for; matrix products, arithmetic and copies ran while one was open for 1% of the time, Pallas kernels for 6%

commit v1 on v0

--- a/solution.py
+++ b/solution.py
@@ -23,7 +23,7 @@
             j = 8 * high + low - 1
             if 0 <= j < TAPS:
                 row = TAPS - 1 - j if reverse else j
-                term = taps[row : row + 1, cols] * shifted[8 * high : 8 * high + FRAMES]
+                term = taps[0, row : row + 1, cols] * shifted[8 * high : 8 * high + FRAMES]
                 total = term if total is None else total + term
     return total
 
@@ -47,7 +47,7 @@
     return (rows < length).astype(jnp.float32)
 
 
-def forward_kernel(tick, info, recv, subs, weight, taps, gain, *rest):
+def forward_kernel(tick, sections, info, recv, subs, weight, taps, gain, *rest):
     out, conv_all, norm_all, inv_all, hid_all, block_in, padded, total = rest[-8:]
     section = info[0]
     slot = tick - section
@@ -93,8 +93,7 @@
                 hid_all[slot, :, cols], weight[cols, :], preferred_element_type=jnp.float32
             )
 
-        def one_chunk(chunk, carry):
-            project(jnp.maximum(chunk - 1, 0))
+        def one_chunk(chunk):
             for step in range(BLOCK // LANES):
                 cols = lane_tile(chunk * (BLOCK // LANES) + step)
                 normed = (block_in[:, cols].astype(jnp.float32) - centre) * inv_std
@@ -103,14 +102,28 @@
                 conv = taps_sum(padded.at[step], taps, cols, False)
                 conv_all[slot, :, cols] = conv
                 hid_all[slot, :, cols] = (conv / (1.0 + jnp.exp(-conv))).astype(jnp.bfloat16)
-            return carry
-
-        lax.fori_loop(0, chunks, one_chunk, 0)
-        project(chunks - 1)
-        out[...] = total[...].astype(jnp.bfloat16)
-
-
-def forward_call(tick, info, recv, subs, weight, taps, gain, stash):
+
+        @pl.when(section != sections - 1)
+        def _():
+            def with_project(chunk, carry):
+                project(jnp.maximum(chunk - 1, 0))
+                one_chunk(chunk)
+                return carry
+
+            lax.fori_loop(0, chunks, with_project, 0)
+            project(chunks - 1)
+            out[...] = total[...].astype(jnp.bfloat16)
+
+        @pl.when(section == sections - 1)
+        def _():
+            def without(chunk, carry):
+                one_chunk(chunk)
+                return carry
+
+            lax.fori_loop(0, chunks, without, 0)
+
+
+def forward_call(tick, sections, info, recv, subs, weight, taps, gain, stash):
     groups, _, width = subs.shape
     f32, bf16 = jnp.float32, jnp.bfloat16
     shapes = (
@@ -124,7 +137,7 @@
     vmem = pl.BlockSpec(memory_space=pltpu.VMEM)
     held = () if stash is None else tuple(stash)
     res = pl.pallas_call(
-        functools.partial(forward_kernel, tick),
+        functools.partial(forward_kernel, tick, sections),
         out_shape=shapes,
         in_specs=[smem] + [vmem] * (5 + len(held)),
         out_specs=(vmem,) * 5,
@@ -136,23 +149,26 @@
         input_output_aliases={6 + i: 1 + i for i in range(len(held))},
         compiler_params=pltpu.CompilerParams(vmem_limit_bytes=VMEM),
         cost_estimate=pl.CostEstimate(
-            flops=8 * FRAMES * width * width, bytes_accessed=width * width * 2, transcendentals=0
+            flops=10**6, bytes_accessed=2**10, transcendentals=0
         ),
         name="section_forward",
     )(info, recv, subs, weight, taps, gain, *held)
     return res[0], res[1:]
 
 
-def backward_kernel(tick, sections, info, recv, seeds, weight, taps, gain, conv_all, norm_all, inv_all, *rest):
+def backward_kernel(tick, sections, info, seeds, recv, crossed, weight, taps, gain, conv_all, norm_all, inv_all, *rest):
     out, grad_all, gconv_all, gain_all = rest[-10:-6]
     grad_out, padded, scaled_now, ahead, mean_sum, dot_sum = rest[-6:]
     section = info[0]
-    slot = tick - (sections - 1 - section)
+    late = jnp.where(section < sections // 2, 1, 0)
+    slot = tick - (sections - 1 - section) - late
     width = out.shape[1]
     tiles = width // LANES
     chunks = width // BLOCK
 
-    @pl.when((slot >= 0) & (slot < seeds.shape[0]))
+    groups = grad_all.shape[0]
+
+    @pl.when((slot >= 0) & (slot < groups))
     def _():
         mask = frame_rows(info[1 + slot])
 
@@ -166,7 +182,11 @@
 
             lax.fori_loop(0, tiles, seed, 0)
 
-        @pl.when(section != sections - 1)
+        @pl.when(section == sections // 2 - 1)
+        def _():
+            grad_out[...] = crossed[...]
+
+        @pl.when((section != sections - 1) & (section != sections // 2 - 1))
         def _():
             grad_out[...] = recv[...]
 
@@ -226,8 +246,8 @@
         lax.fori_loop(0, tiles, finish, 0, unroll=2)
 
 
-def backward_call(tick, sections, info, recv, seeds, weight, taps, gain, stash, held):
-    groups, _, width = seeds.shape
+def backward_call(tick, sections, info, seeds, recv, crossed, weight, taps, gain, stash, held):
+    groups, _, width = stash[0].shape
     f32, bf16 = jnp.float32, jnp.bfloat16
     shapes = (
         jax.ShapeDtypeStruct((FRAMES, width), bf16),
@@ -241,7 +261,7 @@
     res = pl.pallas_call(
         functools.partial(backward_kernel, tick, sections),
         out_shape=shapes,
-        in_specs=[smem] + [vmem] * (8 + len(held)),
+        in_specs=[smem] + [vmem] * (9 + len(held)),
         out_specs=(vmem,) * 4,
         scratch_shapes=[
             pltpu.VMEM((FRAMES, width), bf16),
@@ -251,19 +271,21 @@
             pltpu.VMEM((FRAMES, LANES), f32),
             pltpu.VMEM((FRAMES, LANES), f32),
         ],
-        input_output_aliases={9 + i: 1 + i for i in range(len(held))},
+        input_output_aliases={10 + i: 1 + i for i in range(len(held))},
         compiler_params=pltpu.CompilerParams(vmem_limit_bytes=VMEM),
         cost_estimate=pl.CostEstimate(
-            flops=8 * FRAMES * width * width, bytes_accessed=width * width * 2, transcendentals=0
+            flops=10**6, bytes_accessed=2**10, transcendentals=0
         ),
         name="section_backward",
-    )(info, recv, seeds, weight, taps, gain, *stash[:3], *held)
+    )(info, seeds, recv, crossed, weight, taps, gain, *stash[:3], *held)
     return res[0], res[1:]
 
 
 def taps_kernel(tick, sections, info, gconv_all, norm_all, gain, gain_all, *rest):
     out, padded = rest[-2:]
-    slot = tick - (sections - 1 - info[0])
+    groups = gconv_all.shape[0]
+    late = jnp.where(info[0] >= sections // 2, groups, 1)
+    slot = tick - (sections - 1 - info[0]) - late
     width = out.shape[1]
     if len(rest) == 2:
         out[...] = jnp.zeros(out.shape, jnp.float32)
@@ -293,7 +315,7 @@
         lax.fori_loop(0, width // LANES, one_tile, 0)
 
 
-def on_chip(kernel, name, shapes, operands, scratch=(), aliases=None, flops=10**9, hbm_out=()):
+def on_chip(kernel, name, shapes, operands, scratch=(), aliases=None, hbm_out=()):
     vmem = pl.BlockSpec(memory_space=pltpu.VMEM)
     smem = pl.BlockSpec(memory_space=pltpu.SMEM)
     anywhere = pl.BlockSpec(memory_space=pl.ANY)
@@ -307,7 +329,7 @@
         scratch_shapes=list(scratch),
         input_output_aliases=aliases,
         compiler_params=pltpu.CompilerParams(vmem_limit_bytes=VMEM),
-        cost_estimate=pl.CostEstimate(flops=flops, bytes_accessed=2**20, transcendentals=0),
+        cost_estimate=pl.CostEstimate(flops=10**6, bytes_accessed=2**10, transcendentals=0),
         name=name,
     )(*operands)
 
@@ -328,9 +350,8 @@
 EXTRA = 8
 
 
-def part_kernel(own, info, hid_all, grad_all, sums, out):
-    ring, sides, rows, width = out.shape
-    cut = rows - EXTRA
+def part_kernel(own, info, hid_all, grad_all, out):
+    ring, sides, cut, width = out.shape
     half = info[5] if own else 1 - info[5]
     piece = 8 * cut
     tokens = hid_all.shape[0] * FRAMES
@@ -343,53 +364,42 @@
         )
         for i in range(piece // cut):
             block = step * (piece // cut) + i
-            out[block // sides, block % sides, 0:cut] = part[i * cut : (i + 1) * cut].astype(
-                jnp.bfloat16
-            )
-    rest = jnp.zeros((EXTRA - 1, width), jnp.float32)
-    for block in range(ring * sides):
-        row = sums[pl.ds(half * (ring * sides) + block, 1), :]
-        out[block // sides, block % sides, cut:] = jnp.concatenate([row, rest], axis=0).astype(
-            jnp.bfloat16
-        )
-
-
-def merge_kernel(info, mine, other, own, *sends):
-    ring = mine.shape[0]
-    place, side = info[6], info[7]
+            out[block // sides, block % sides] = part[i * cut : (i + 1) * cut].astype(jnp.bfloat16)
+
+
+def ring_kernel(step, info, mine, other, sums, sums_other, *rest):
+    ring, sides, cut, width = mine.shape
+    core, place, side = info[5], info[6], info[7]
     ahead, behind = ring // 2, ring - 1 - ring // 2
-
-    def add(owner, x):
+    f32 = jnp.float32
+    blank = jnp.zeros((EXTRA - 1, width), f32)
+
+    def fill(target, owner, x, *more):
         owner = owner % ring
-        return (mine[owner, x].astype(jnp.float32) + other[owner, x].astype(jnp.float32)).astype(
-            jnp.bfloat16
-        )
-
-    for step, send in enumerate(sends):
-        send[0] = add(place + ahead - step, 1 - side)
-        send[1] = add(place + ring - behind + step, 1 - side)
-    for owner in range(ring):
-        own[owner] = add(owner, side)
-
-
-def ring_kernel(step, info, own, crossed, *rest):
-    ring = own.shape[0]
-    place = info[6]
-    ahead, behind = ring // 2, ring - 1 - ring // 2
-    up = own[(place + ahead - step) % ring].astype(jnp.float32) + crossed[0].astype(jnp.float32)
-    down = own[(place + ring - behind + step) % ring].astype(jnp.float32) + crossed[1].astype(
-        jnp.float32
-    )
-    if len(rest) == 4:
-        up = up + rest[0][...].astype(jnp.float32)
-        down = down + rest[1][...].astype(jnp.float32)
-    rest[-2][...] = up.astype(rest[-2].dtype)
-    rest[-1][...] = down.astype(rest[-1].dtype)
-
-
-def place_kernel(ring, sources, count, info, *rest):
+        total = mine[owner, x].astype(f32) + other[owner, x].astype(f32)
+        index = pl.ds((core * ring + owner) * sides + x, 1)
+        edge = jnp.concatenate([sums[index, :] + sums_other[index, :], blank], axis=0)
+        for block in more:
+            total = total + block[:cut].astype(f32)
+            edge = edge + block[cut:].astype(f32)
+        target[:cut] = total.astype(target.dtype)
+        target[cut:] = edge.astype(target.dtype)
+
+    if step < 0:
+        for i in range(ahead):
+            fill(rest[i].at[0], place + ahead - i, 1 - side)
+            fill(rest[i].at[1], place + ring - behind + i, 1 - side)
+        return
+    crossed, arrived = rest[0], rest[1:-2]
+    up, down = rest[-2:]
+    fill(up, place + ahead - step, side, crossed[0], *arrived[:1])
+    fill(down, place + ring - behind + step, side, crossed[1], *arrived[1:])
+
+
+def place_kernel(ring, sources, count, last, info, *rest):
     blocks = rest[:count]
-    whole, edge, sems = rest[-3:]
+    whole, edge = rest[-5:-3] if last else rest[-3:-1]
+    sems = rest[-1]
     core, place, side = info[5], info[6], info[7]
     cut = blocks[0].shape[-2] - EXTRA
     copies = []
@@ -405,6 +415,11 @@
         copy.start()
         copies.append(copy)
         edge[index] = block[cut:, :].astype(jnp.float32)
+    if last:
+        taps_out, gain_out = rest[-3:-1]
+        for row in range(TAPS):
+            taps_out[0, row : row + 1, :] = edge[row, 0:1, :]
+        gain_out[...] = edge[TAPS, 0:1, :]
     for copy in copies:
         copy.wait()
 
@@ -419,9 +434,10 @@
         sources.append((which[0], i, offset, core_flip, side_flip))
     count = len(blocks)
     return on_chip(
-        functools.partial(place_kernel, ring, sources, count),
+        functools.partial(place_kernel, ring, sources, count, held is not None),
         "place_sums",
-        [(shape, jnp.bfloat16), ((4 * ring, EXTRA, shape[1]), jnp.float32)],
+        [(shape, jnp.bfloat16), ((4 * ring, EXTRA, shape[1]), jnp.float32)]
+        + ([((1, TAPS, shape[1]), jnp.float32), ((1, shape[1]), jnp.float32)] if held else []),
         (info, *blocks, *(held or ())),
         [pltpu.SemaphoreType.DMA((len(sources),))],
         {count + 1: 0, count + 2: 1} if held else {},
@@ -453,73 +469,77 @@
         return on_chip(
             functools.partial(part_kernel, own),
             "weight_part",
-            [((ring, 2, rows, width), bf16)],
-            (info, hidden, grads, sums),
-            flops=4 * 10**9,
+            [((ring, 2, cut, width), bf16)],
+            (info, hidden, grads),
         )[0]
 
-    swapped = to_core(part(False))
+    other = to_core(part(False))
+    sums = sums()
+    sums_other = to_core(sums)
     mine = part(True)
     ahead, behind = ring // 2, ring - 1 - ring // 2
-    merged = on_chip(
-        merge_kernel,
-        "merge_cores",
-        [((ring, rows, width), bf16)] + [((2, rows, width), bf16)] * ahead,
-        (info, mine, swapped),
-    )
-    own, crossed = merged[0], [to_x(send) for send in merged[1:]]
-    up = down = None
-    for step in range(ahead):
-        arrived = () if step == 0 else (up, down)
-        last = step == ahead - 1
-        up, down = on_chip(
+    block, pair = ((rows, width), bf16), ((2, rows, width), bf16)
+
+    def ring_call(step, *arrived):
+        shapes = [block, ((rows, width), f32) if step == ahead - 1 else block]
+        return on_chip(
             functools.partial(ring_kernel, step),
             "ring_step",
-            [((rows, width), bf16), ((rows, width), f32 if last else bf16)],
-            (info, own, crossed[step], *arrived),
+            shapes if step >= 0 else [pair] * ahead,
+            (info, mine, other, sums, sums_other, *arrived),
         )
+
+    crossed = [to_x(send) for send in ring_call(-1)]
+    arrived = ()
+    for step in range(ahead):
+        up, down = ring_call(step, crossed[step], *arrived)
         up = along_z(up, 1)
-        if not last:
+        if step < ahead - 1:
             down = along_z(down, -1)
+        arrived = (up, down)
     done = (down + up.astype(f32)).astype(bf16)
 
     ups, downs = [done], [done]
-    pieces = []
-
-    def spread(blocks, offsets):
-        stack = jnp.stack(blocks) if len(blocks) > 1 else blocks[0]
-        index = range(len(blocks)) if len(blocks) > 1 else [None]
-        crossed = to_x(stack)
-        for array, core_flip, side_flip in (
-            (stack, False, False),
-            (crossed, False, True),
-            (to_core(stack), True, False),
-            (to_core(crossed), True, True),
-        ):
-            for i, offset in zip(index, offsets):
-                pieces.append((array, i, offset, core_flip, side_flip))
-
+    stacks, swaps, tags = [], [], []
     for step in range(1, ahead + 1):
         ups.append(along_z(ups[-1], 1))
         if step <= behind:
             downs.append(along_z(downs[-1], -1))
+        if step > 1:
+            swaps.append(to_x(stacks[-1]))
+        fresh = [(-step, ups[step])] + ([(step, downs[step])] if step <= behind else [])
         if step == 1:
-            spread([done, ups[1], downs[1]], [0, -1, 1])
-        elif step <= behind:
-            spread([ups[step], downs[step]], [-step, step])
-            if step == behind - 1:
-                early = place_call(info, pieces, (width, width), ring, None)
-                pieces.clear()
-        else:
-            spread([ups[step]], [-step])
-    whole, edge = place_call(info, pieces, (width, width), ring, early)
-    edge = edge[:, 0]
-    return whole, edge[:TAPS], edge[TAPS:]
+            fresh = [(0, done)] + fresh
+        tags.append([offset for offset, _ in fresh])
+        stacks.append(jnp.stack([piece for _, piece in fresh]))
+    swaps.append(to_x(stacks[-1]))
+
+    def batch(groups):
+        joined = jnp.concatenate([stack for stack, _, _ in groups])
+        turned = to_core(joined)
+        pieces = []
+        count = 0
+        for stack, offsets, side_flip in groups:
+            for i, offset in enumerate(offsets):
+                pieces.append((stack, i, offset, False, side_flip))
+                pieces.append((turned, count, offset, True, side_flip))
+                count += 1
+        return pieces
+
+    early = [(stacks[i], tags[i], False) for i in range(behind)]
+    early += [(swaps[i], tags[i], True) for i in range(behind - 1)]
+    middle = [(stacks[behind], tags[behind], False), (swaps[behind - 1], tags[behind - 1], True)]
+    late = [(swaps[behind], tags[behind], True)]
+    held = place_call(info, batch(early), (width, width), ring, None)
+    whole, _, taps_sums, gain_sum = place_call(
+        info, batch(middle + late), (width, width), ring, held
+    )
+    return whole, taps_sums, gain_sum
 
 
 def body(mels, lengths, sub_weight, block_weight, conv_kernel, norm_gain, cotangent):
     weight = block_weight[0]
-    taps = conv_kernel[0]
+    taps = conv_kernel
     gain = norm_gain
     width = cotangent.shape[1]
     groups = lengths.shape[0]
@@ -568,32 +588,42 @@
     turn = sections - 1
     ticks = turn + groups
     stash = held = sums = None
-    fwd_recv = {}
-    bwd_recv = {}
     idle = jnp.zeros((FRAMES, width), jnp.bfloat16)
-    for tick in range(turn + ticks):
+    forward_recv = backward_recv = idle
+
+    half = sections // 2
+    crossed = {}
+    for tick in range(turn + ticks + 1):
+        back = tick - turn
         if tick < ticks:
             block, stash = forward_call(
-                tick, info, fwd_recv.pop(tick - 1, idle), subs, weight, taps, gain, stash
+                tick, sections, info, forward_recv, subs, weight, taps, gain, stash
             )
             pairs = [(s, s + 1) for s in range(sections - 1) if 0 <= tick - s < groups]
-            if pairs:
-                fwd_recv[tick] = relay(block, pairs)
-        back = tick - turn
-        if back >= 0:
-            block, held = backward_call(
-                back, sections, info, bwd_recv.pop(back - 1, idle), seeds, weight, taps, gain, stash, held
-            )
-            pairs = [
-                (s, s - 1)
-                for s in range(1, sections)
-                if 0 <= back - (sections - 1 - s) < groups
-            ]
-            if pairs:
-                bwd_recv[back] = relay(block, pairs)
+            forward_recv = relay(block, pairs) if pairs else idle
+        if back < 0:
+            continue
+        block, held = backward_call(
+            back, sections, info, seeds, backward_recv, crossed.get(back - 2, idle),
+            weight, taps, gain, stash, held,
+        )
+        active = [
+            s
+            for s in range(1, sections)
+            if 0 <= back - (sections - 1 - s) - (1 if s < half else 0) < groups
+        ]
+        pairs = [(s, s - 1) for s in active if s != half]
+        backward_recv = relay(block, pairs) if pairs else idle
+        if half in active:
+            crossed[back] = relay(block, [(half, half - 1)])
+        if groups <= back < ticks:
             sums = taps_call(back, sections, info, held, stash, gain, sums)
-    weight_sum, taps_sums, gain_sum = column_sum(info, stash[3], held[0], sums, shards)
-    return (weight_sum[None], taps_sums[None], gain_sum)
+
+    def last_sums():
+        return taps_call(ticks, sections, info, held, stash, gain, sums)
+
+    weight_sum, taps_sums, gain_sum = column_sum(info, stash[3], held[0], last_sums, shards)
+    return (weight_sum[None], taps_sums, gain_sum)
 
 
 def solution(mesh):

time: 368 us -> 364 us (0.989)
  starting transfers between devices: 96.1 us -> 81.7 us
  Pallas kernels: 68.1 us -> 76.3 us
    ppermute x14, waiting for transfers between devices: 14.8 us -> 33.8 us  [along_z(): return lax.ppermute(block, 'dp', route)]
    ppermute x9 -> x4, starting transfers between devices: 38.1 us -> 27.4 us  [to_core(): return lax.ppermute(block, 'dp', [(d, d ^ 1) for d in range(shards)])]
    ppermute x8, waiting for transfers between devices: 27.4 us -> 16.9 us  [to_x(): lax.ppermute(block, 'dp', [(d, (d + shards // 2) % shards) for d in range...]
    pallas_call x11 -> x12, Pallas kernels: 24.3 us -> 34.1 us  [backward_call(): pl.pallas_call(functools.partial(backward_kernel, tick, sections), out_sh...]
    ppermute x8, starting transfers between devices: 13.5 us -> 3.75 us  [to_x(): lax.ppermute(block, 'dp', [(d, (d + shards // 2) % shards) for d in range...]
    ppermute x20 -> x25, waiting for transfers between devices: 147 us -> 143 us  [relay(): return lax.ppermute(block, ('dp', 'section'), route)]
    ppermute x20 -> x25, starting transfers between devices: 26.2 us -> 29.6 us  [relay(): return lax.ppermute(block, ('dp', 'section'), route)]
    pallas_call x20 -> x17, Pallas kernels: 25.5 us -> 23.9 us  [on_chip(): pl.pallas_call(kernel, out_shape=tuple((jax.ShapeDtypeStruct(shape, dtype...]
  transfers between devices with their start and end apart: 53 -> 53, of which waited for: 20 -> 22; matrix products, arithmetic and copies ran while one was open for 1% -> 1% of each run, Pallas kernels for 6% -> 7%
where the time goes in v1:
time: 364 us; the launch traced here: 359 us
  waiting for transfers between devices  194 us (53%)
  starting transfers between devices  81.7 us (22%)
  Pallas kernels  76.3 us (21%)
  local copies, waits for them, and re-layouts  5.41 us (1%)
    ppermute x25, waiting for transfers between devices, relay(): return lax.ppermute(block, ('dp', 'section'), route)  143 us
    pallas_call x12, Pallas kernels, backward_call(): pl.pallas_call(functools.partial(backward_kernel, tick, sections), out_sh...  34.1 us
    ppermute x14, waiting for transfers between devices, along_z(): return lax.ppermute(block, 'dp', route)  33.8 us
    ppermute x25, starting transfers between devices, relay(): return lax.ppermute(block, ('dp', 'section'), route)  29.6 us
    ppermute x4, starting transfers between devices, to_core(): return lax.ppermute(block, 'dp', [(d, d ^ 1) for d in range(shards)])  27.4 us
    pallas_call x17, Pallas kernels, on_chip(): pl.pallas_call(kernel, out_shape=tuple((jax.ShapeDtypeStruct(shape, dtype...  23.9 us
    ppermute x14, starting transfers between devices, along_z(): return lax.ppermute(block, 'dp', route)  19.4 us
    pallas_call x11, Pallas kernels, forward_call(): pl.pallas_call(functools.partial(forward_kernel, tick, sections), out_sha...  18.3 us
  transfers between devices with their start and end apart: 53, of which 22 were waited for; matrix products, arithmetic and copies ran while one was open for 1% of the time, Pallas kernels for 7%

profile of v1, /device:TPU:1, one launch (start us, length us, event | category | flops | bytes accessed | tf_op | source)
XLA Modules:
  0.0 359.5 jit_solution(5783633232345880353)
XLA Ops:
  1.5 0.9 copy.92.taps
  2.5 1.0 reshape.19
  4.1 2.3 copy-done.1
  6.5 3.4 section_forward.11
  9.9 1.4 collective-permute-start.1
  11.3 3.6 %collective-permute-done.1.recv = bf16[96,1536]{1,0:T(8,128)(2,1)S(1)} collective-permute-done((bf16[96,1536]{1,0:T(8,128)(2,1)S(1)}, bf16[96,1536]{1,0:T(8,128)(2,1)S(1)}, u32[]{:S(2)}, u32[]{:S(2)}) %collective-permute-start.1) | collective-permute-done | bytes 294944 | tf_op jit(solution)/shard_map/ppermute | solution.py:564
  15.0 3.4 section_forward.12
  18.4 3.8 %collective-permute-start.2 = (bf16[96,1536]{1,0:T(8,128)(2,1)S(1)}, bf16[96,1536]{1,0:T(8,128)(2,1)S(1)}, u32[]{:S(2)}, u32[]{:S(2)}) collective-permute-start(bf16[96,1536]{1,0:T(8,128)(2,1)S(1)} %get-tuple-element.126), channel_id=1, source_target_pairs={{0,1},{8,9},{16,17},{24,25},{32,33},{40,41},{48,49},{56,57},{64,65... | collective-permute-start | bytes 884744 | tf_op jit(solution)/shard_map/ppermute | solution.py:564
  22.2 3.6 %collective-permute-done.2.recv = bf16[96,1536]{1,0:T(8,128)(2,1)S(1)} collective-permute-done((bf16[96,1536]{1,0:T(8,128)(2,1)S(1)}, bf16[96,1536]{1,0:T(8,128)(2,1)S(1)}, u32[]{:S(2)}, u32[]{:S(2)}) %collective-permute-start.2) | collective-permute-done | bytes 294944 | tf_op jit(solution)/shard_map/ppermute | solution.py:564
  25.9 3.4 section_forward.13
  29.3 3.8 %collective-permute-start.3 = (bf16[96,1536]{1,0:T(8,128)(2,1)S(1)}, bf16[96,1536]{1,0:T(8,128)(2,1)S(1)}, u32[]{:S(2)}, u32[]{:S(2)}) collective-permute-start(bf16[96,1536]{1,0:T(8,128)(2,1)S(1)} %get-tuple-element.131), channel_id=1, source_target_pairs={{0,1},{8,9},{16,17},{24,25},{32,33},{40,41},{48,49},{56,57},{64,65... | collective-permute-start | bytes 884744 | tf_op jit(solution)/shard_map/ppermute | solution.py:564
  33.1 3.6 %collective-permute-done.3.recv = bf16[96,1536]{1,0:T(8,128)(2,1)S(1)} collective-permute-done((bf16[96,1536]{1,0:T(8,128)(2,1)S(1)}, bf16[96,1536]{1,0:T(8,128)(2,1)S(1)}, u32[]{:S(2)}, u32[]{:S(2)}) %collective-permute-start.3) | collective-permute-done | bytes 294944 | tf_op jit(solution)/shard_map/ppermute | solution.py:564
  36.8 3.4 section_forward.14
  40.2 3.8 %collective-permute-start.4 = (bf16[96,1536]{1,0:T(8,128)(2,1)S(1)}, bf16[96,1536]{1,0:T(8,128)(2,1)S(1)}, u32[]{:S(2)}, u32[]{:S(2)}) collective-permute-start(bf16[96,1536]{1,0:T(8,128)(2,1)S(1)} %get-tuple-element.136), channel_id=1, source_target_pairs={{0,1},{8,9},{16,17},{24,25},{32,33},{40,41},{48,49},{56,57},{64,65... | collective-permute-start | bytes 884744 | tf_op jit(solution)/shard_map/ppermute | solution.py:564
  44.8 2.9 collective-permute-done.4.recv
  59.3 1.3 section_forward.21
  70.6 1.3 collective-permute-start.22
  72.5 102.1 %collective-permute-done.22.recv = bf16[96,1536]{1,0:T(8,128)(2,1)S(1)} collective-permute-done((bf16[96,1536]{1,0:T(8,128)(2,1)S(1)}, bf16[96,1536]{1,0:T(8,128)(2,1)S(1)}, u32[]{:S(2)}, u32[]{:S(2)}) %collective-permute-start.22) | collective-permute-done | bytes 294944 | tf_op jit(solution)/shard_map/ppermute | solution.py:564
  174.6 4.9 %section_backward.20 = (bf16[96,1536]{1,0:T(8,128)(2,1)S(1)}, bf16[4,96,1536]{2,1,0:T(8,128)(2,1)S(1)}, f32[4,96,1536]{2,1,0:T(8,128)S(1)}, f32[4,8,1536]{2,1,0:T(8,128)S(1)}) custom-call(s32[8]{0:T(128)S(1)} %concatenate.10.info, bf16[4,96,1536]{2,1,0:T(8,128)(2,1)S(1)} %bitcast.67, ...), custom_call_target="tpu_custom_call", output_to_operand_aliasing={{1}: (10, {}), {2}: (11, {}), {3}: (12, {})} | custom-call | flops 1000000 | bytes 1024 | tf_op jit(solution)/shard_map/section_backward/pallas_call | solution.py:261
  179.6 1.3 collective-permute-start.24
  180.9 2.3 taps_gradient.12.rest_0_
  183.2 17.5 %collective-permute-done.24.recv = bf16[96,1536]{1,0:T(8,128)(2,1)S(1)} collective-permute-done((bf16[96,1536]{1,0:T(8,128)(2,1)S(1)}, bf16[96,1536]{1,0:T(8,128)(2,1)S(1)}, u32[]{:S(2)}, u32[]{:S(2)}) %collective-permute-start.24) | collective-permute-done | bytes 294944 | tf_op jit(solution)/shard_map/ppermute | solution.py:564
  200.7 4.9 %section_backward.21 = (bf16[96,1536]{1,0:T(8,128)(2,1)S(1)}, bf16[4,96,1536]{2,1,0:T(8,128)(2,1)S(1)}, f32[4,96,1536]{2,1,0:T(8,128)S(1)}, f32[4,8,1536]{2,1,0:T(8,128)S(1)}) custom-call(s32[8]{0:T(128)S(1)} %concatenate.10.info, bf16[4,96,1536]{2,1,0:T(8,128)(2,1)S(1)} %bitcast.68, ...), custom_call_target="tpu_custom_call", output_to_operand_aliasing={{1}: (10, {}), {2}: (11, {}), {3}: (12, {})} | custom-call | flops 1000000 | bytes 1024 | tf_op jit(solution)/shard_map/section_backward/pallas_call | solution.py:261
  205.6 1.3 collective-permute-start.25
  206.9 2.3 taps_gradient.13.rest_0_
  209.3 5.5 %collective-permute-done.25.recv = bf16[96,1536]{1,0:T(8,128)(2,1)S(1)} collective-permute-done((bf16[96,1536]{1,0:T(8,128)(2,1)S(1)}, bf16[96,1536]{1,0:T(8,128)(2,1)S(1)}, u32[]{:S(2)}, u32[]{:S(2)}) %collective-permute-start.25) | collective-permute-done | bytes 294944 | tf_op jit(solution)/shard_map/ppermute | solution.py:564
  214.8 4.9 %section_backward.22 = (bf16[96,1536]{1,0:T(8,128)(2,1)S(1)}, bf16[4,96,1536]{2,1,0:T(8,128)(2,1)S(1)}, f32[4,96,1536]{2,1,0:T(8,128)S(1)}, f32[4,8,1536]{2,1,0:T(8,128)S(1)}) custom-call(s32[8]{0:T(128)S(1)} %concatenate.10.info, bf16[4,96,1536]{2,1,0:T(8,128)(2,1)S(1)} %bitcast.69, ...), custom_call_target="tpu_custom_call", output_to_operand_aliasing={{1}: (10, {}), {2}: (11, {}), {3}: (12, {})} | custom-call | flops 1000000 | bytes 1024 | tf_op jit(solution)/shard_map/section_backward/pallas_call | solution.py:261
  219.7 1.3 collective-permute-start.26
  221.0 2.3 taps_gradient.14.rest_0_
  223.4 3.8 %collective-permute-done.26.recv = bf16[96,1536]{1,0:T(8,128)(2,1)S(1)} collective-permute-done((bf16[96,1536]{1,0:T(8,128)(2,1)S(1)}, bf16[96,1536]{1,0:T(8,128)(2,1)S(1)}, u32[]{:S(2)}, u32[]{:S(2)}) %collective-permute-start.26) | collective-permute-done | bytes 294944 | tf_op jit(solution)/shard_map/ppermute | solution.py:564
  227.2 14.6 %section_backward.23 = (bf16[96,1536]{1,0:T(8,128)(2,1)}, bf16[4,96,1536]{2,1,0:T(8,128)(2,1)S(1)}, f32[4,96,1536]{2,1,0:T(8,128)S(1)}, f32[4,8,1536]{2,1,0:T(8,128)S(1)}) custom-call(s32[8]{0:T(128)S(1)} %concatenate.10.info, bf16[4,96,1536]{2,1,0:T(8,128)(2,1)S(1)} %bitcast.70, ...), custom_call_target="tpu_custom_call", output_to_operand_aliasing={{1}: (10, {}), {2}: (11, {}), {3}: (12, {})} | custom-call | flops 1000000 | bytes 1024 | tf_op jit(solution)/shard_map/section_backward/pallas_call | solution.py:261
  241.8 2.0 weight_part.3
  243.8 17.7 %collective-permute-start.27 = (bf16[8,2,48,1536]{3,2,1,0:T(8,128)(2,1)S(1)}, bf16[8,2,48,1536]{3,2,1,0:T(8,128)(2,1)S(1)}, u32[]{:S(2)}, u32[]{:S(2)}) collective-permute-start(bf16[8,2,48,1536]{3,2,1,0:T(8,128)(2,1)S(1)} %weight_part.3), channel_id=1, source_target_pairs={{0,8},{8,0},{16,24},{24,16},{32,40},{40,32},{48,56},{56,48},{64,72... | collective-permute-start | bytes 7077896 | tf_op jit(solution)/shard_map/ppermute | solution.py:463
  261.5 2.3 taps_gradient.15.sums
  263.9 2.0 weight_part.2.mine
  265.9 0.9 ring_step.5
  266.9 1.5 collective-permute-start.31
  268.3 7.7 %collective-permute-done.32.rest_0_ = bf16[2,56,1536]{2,1,0:T(8,128)(2,1)S(1)} collective-permute-done((bf16[2,56,1536]{2,1,0:T(8,128)(2,1)S(1)}, bf16[2,56,1536]{2,1,0:T(8,128)(2,1)S(1)}, u32[]{:S(2)}, u32[]{:S(2)}) %collective-permute-start.32) | collective-permute-done | bytes 344096 | tf_op jit(solution)/shard_map/ppermute | solution.py:466
  276.7 1.6 collective-permute-start.33
  278.3 4.0 %collective-permute-start.34 = (bf16[56,1536]{1,0:T(8,128)(2,1)S(1)}, bf16[56,1536]{1,0:T(8,128)(2,1)S(1)}, u32[]{:S(2)}, u32[]{:S(2)}) collective-permute-start(bf16[56,1536]{1,0:T(8,128)(2,1)S(1)} %get-tuple-element.227), channel_id=1, source_target_pairs={{0,112},{8,120},{16,0},{24,8},{32,16},{40,24},{48,32},{56,40},{64,... | collective-permute-start | bytes 516104 | tf_op jit(solution)/shard_map/ppermute | solution.py:460
  283.4 1.6 collective-permute-done.33.rest_1_
  285.9 3.9 %collective-permute-start.36 = (bf16[56,1536]{1,0:T(8,128)(2,1)S(1)}, bf16[56,1536]{1,0:T(8,128)(2,1)S(1)}, u32[]{:S(2)}, u32[]{:S(2)}) collective-permute-start(bf16[56,1536]{1,0:T(8,128)(2,1)S(1)} %get-tuple-element.229), channel_id=1, source_target_pairs={{0,112},{8,120},{16,0},{24,8},{32,16},{40,24},{48,32},{56,40},{64,... | collective-permute-start | bytes 516104 | tf_op jit(solution)/shard_map/ppermute | solution.py:460
  290.1 2.4 collective-permute-done.35.rest_1_
  293.2 1.4 collective-permute-start.37
  294.6 2.5 collective-permute-start.38
  297.1 2.7 collective-permute-done.37.rest_1_
  300.6 1.2 collective-permute-start.39
  301.7 5.5 %collective-permute-done.39 = bf16[56,1536]{1,0:T(8,128)(2,1)S(1)} collective-permute-done((bf16[56,1536]{1,0:T(8,128)(2,1)S(1)}, bf16[56,1536]{1,0:T(8,128)(2,1)S(1)}, u32[]{:S(2)}, u32[]{:S(2)}) %collective-permute-start.39) | collective-permute-done | bytes 172064 | tf_op jit(solution)/shard_map/ppermute | solution.py:460
  307.2 1.7 collective-permute-start.44
  309.0 2.8 collective-permute-done.44
  311.8 2.6 collective-permute-done.40
  314.9 1.5 collective-permute-start.41
  316.4 3.0 collective-permute-done.45
  319.5 1.3 collective-permute-done.41
  321.7 1.5 collective-permute-start.42
  323.2 4.9 %collective-permute-done.42 = bf16[56,1536]{1,0:T(8,128)(2,1)S(1)} collective-permute-done((bf16[56,1536]{1,0:T(8,128)(2,1)S(1)}, bf16[56,1536]{1,0:T(8,128)(2,1)S(1)}, u32[]{:S(2)}, u32[]{:S(2)}) %collective-permute-start.42) | collective-permute-done | bytes 172064 | tf_op jit(solution)/shard_map/ppermute | solution.py:460
  328.1 2.8 collective-permute-done.51.rest_5_
  330.9 8.2 %collective-permute-start.52 = (bf16[12,56,1536]{2,1,0:T(8,128)(2,1)S(1)}, bf16[12,56,1536]{2,1,0:T(8,128)(2,1)S(1)}, u32[]{:S(2)}, u32[]{:S(2)}) collective-permute-start(bf16[12,56,1536]{2,1,0:T(8,128)(2,1)S(1)} %constant_dynamic-update-slice_fusion), channel_id=1, source_target_pairs={{0,8},{8,0},{16,24},{24,16},{32,40},{40,32},{48,56},{56,48},{64,72... | collective-permute-start | bytes 6193160 | tf_op jit(solution)/shard_map/ppermute | solution.py:463
  339.3 6.9 %collective-permute-done.43 = bf16[56,1536]{1,0:T(8,128)(2,1)S(1)} collective-permute-done((bf16[56,1536]{1,0:T(8,128)(2,1)S(1)}, bf16[56,1536]{1,0:T(8,128)(2,1)S(1)}, u32[]{:S(2)}, u32[]{:S(2)}) %collective-permute-start.43) | collective-permute-done | bytes 172064 | tf_op jit(solution)/shard_map/ppermute | solution.py:460
  346.3 5.7 %collective-permute-done.48.rest_3_ = bf16[1,56,1536]{2,1,0:T(8,128)(2,1)S(1)} collective-permute-done((bf16[1,56,1536]{2,1,0:T(8,128)(2,1)S(1)}, bf16[1,56,1536]{2,1,0:T(8,128)(2,1)S(1)}, u32[]{:S(2)}, u32[]{:S(2)}) %collective-permute-start.48) | collective-permute-done | bytes 172064 | tf_op jit(solution)/shard_map/ppermute | solution.py:466
  352.1 1.5 collective-permute-start.49
  353.6 2.5 place_sums.2
  356.1 2.2 place_sums.3
  358.4 0.9 copy.115
  (114 shorter events, 30.5 us)
Async XLA Ops:
  0.6 2.8 copy-start
  0.6 3.3 copy-start.4
  0.7 3.5 copy-start.3
  0.7 3.3 collective-permute-start
  4.1 2.3 copy-start.1
  6.5 8.5 %copy-start.2 = (bf16[1,1536,1536]{2,1,0:T(8,128)(2,1)S(1)}, bf16[1,1536,1536]{2,1,0:T(8,128)(2,1)}, u32[]{:S(2)}) copy-start(bf16[1,1536,1536]{2,1,0:T(8,128)(2,1)} %param.10) | copy-start | bytes 14155780
  9.9 5.1 %collective-permute-start.1 = (bf16[96,1536]{1,0:T(8,128)(2,1)S(1)}, bf16[96,1536]{1,0:T(8,128)(2,1)S(1)}, u32[]{:S(2)}, u32[]{:S(2)}) collective-permute-start(bf16[96,1536]{1,0:T(8,128)(2,1)S(1)} %get-tuple-element.121), channel_id=1, source_target_pairs={{0,1},{8,9},{16,17},{24,25},{32,33},{40,41},{48,49},{56,57},{64,65... | collective-permute-start | bytes 884744 | tf_op jit(solution)/shard_map/ppermute | solution.py:564
  18.4 7.5 %collective-permute-start.2 = (bf16[96,1536]{1,0:T(8,128)(2,1)S(1)}, bf16[96,1536]{1,0:T(8,128)(2,1)S(1)}, u32[]{:S(2)}, u32[]{:S(2)}) collective-permute-start(bf16[96,1536]{1,0:T(8,128)(2,1)S(1)} %get-tuple-element.126), channel_id=1, source_target_pairs={{0,1},{8,9},{16,17},{24,25},{32,33},{40,41},{48,49},{56,57},{64,65... | collective-permute-start | bytes 884744 | tf_op jit(solution)/shard_map/ppermute | solution.py:564
  29.3 7.5 %collective-permute-start.3 = (bf16[96,1536]{1,0:T(8,128)(2,1)S(1)}, bf16[96,1536]{1,0:T(8,128)(2,1)S(1)}, u32[]{:S(2)}, u32[]{:S(2)}) collective-permute-start(bf16[96,1536]{1,0:T(8,128)(2,1)S(1)} %get-tuple-element.131), channel_id=1, source_target_pairs={{0,1},{8,9},{16,17},{24,25},{32,33},{40,41},{48,49},{56,57},{64,65... | collective-permute-start | bytes 884744 | tf_op jit(solution)/shard_map/ppermute | solution.py:564
  36.8 7.3 %copy-start.5 = (bf16[384,1536]{1,0:T(8,128)(2,1)S(1)}, bf16[384,1536]{1,0:T(8,128)(2,1)}, u32[]{:S(2)}) copy-start(bf16[384,1536]{1,0:T(8,128)(2,1)} %param.13) | copy-start | bytes 3538948
  40.2 7.5 %collective-permute-start.4 = (bf16[96,1536]{1,0:T(8,128)(2,1)S(1)}, bf16[96,1536]{1,0:T(8,128)(2,1)S(1)}, u32[]{:S(2)}, u32[]{:S(2)}) collective-permute-start(bf16[96,1536]{1,0:T(8,128)(2,1)S(1)} %get-tuple-element.136), channel_id=1, source_target_pairs={{0,1},{8,9},{16,17},{24,25},{32,33},{40,41},{48,49},{56,57},{64,65... | collective-permute-start | bytes 884744 | tf_op jit(solution)/shard_map/ppermute | solution.py:564
  44.1 8.6 %collective-permute-start.11 = (bf16[384,1536]{1,0:T(8,128)(2,1)S(1)}, bf16[384,1536]{1,0:T(8,128)(2,1)S(1)}, u32[]{:S(2)}, u32[]{:S(2)}) collective-permute-start(bf16[384,1536]{1,0:T(8,128)(2,1)S(1)} %copy-done.5), channel_id=1, source_target_pairs={{7,135},{15,143},{23,151},{31,159},{39,167},{47,175},{55,183},{63,... | collective-permute-start | bytes 3538952 | tf_op jit(solution)/shard_map/ppermute | solution.py:573
  48.2 0.7 collective-permute-start.5
  49.5 0.7 collective-permute-start.6
  50.8 0.7 collective-permute-start.7
  52.0 2.0 collective-permute-start.8
  53.3 1.9 collective-permute-start.12
  54.5 2.2 collective-permute-start.9
  56.1 1.9 collective-permute-start.13
  57.3 2.0 collective-permute-start.10
  58.6 2.0 collective-permute-start.14
  61.1 1.4 collective-permute-start.15
  61.8 3.2 collective-permute-start.17
  63.1 2.0 collective-permute-start.16
  63.8 3.8 %collective-permute-start.19 = (bf16[96,1536]{1,0:T(8,128)(2,1)S(1)}, bf16[96,1536]{1,0:T(8,128)(2,1)S(1)}, u32[]{:S(2)}, u32[]{:S(2)}) collective-permute-start(bf16[96,1536]{1,0:T(8,128)(2,1)S(1)} %get-tuple-element.191), channel_id=1, source_target_pairs={{4,131},{12,139},{20,147},{28,155},{36,163},{44,171},{52,179},{60,... | collective-permute-start | bytes 884744 | tf_op jit(solution)/shard_map/ppermute | solution.py:564
  65.6 1.9 collective-permute-start.18
  66.3 3.8 %collective-permute-start.21 = (bf16[96,1536]{1,0:T(8,128)(2,1)S(1)}, bf16[96,1536]{1,0:T(8,128)(2,1)S(1)}, u32[]{:S(2)}, u32[]{:S(2)}) collective-permute-start(bf16[96,1536]{1,0:T(8,128)(2,1)S(1)} %get-tuple-element.195), channel_id=1, source_target_pairs={{4,131},{12,139},{20,147},{28,155},{36,163},{44,171},{52,179},{60,... | collective-permute-start | bytes 884744 | tf_op jit(solution)/shard_map/ppermute | solution.py:564
  68.1 1.9 collective-permute-start.20
  68.8 3.7 %collective-permute-start.23 = (bf16[96,1536]{1,0:T(8,128)(2,1)S(1)}, bf16[96,1536]{1,0:T(8,128)(2,1)S(1)}, u32[]{:S(2)}, u32[]{:S(2)}) collective-permute-start(bf16[96,1536]{1,0:T(8,128)(2,1)S(1)} %get-tuple-element.199), channel_id=1, source_target_pairs={{4,131},{12,139},{20,147},{28,155},{36,163},{44,171},{52,179},{60,... | collective-permute-start | bytes 884744 | tf_op jit(solution)/shard_map/ppermute | solution.py:564
  70.6 104.0 %collective-permute-start.22 = (bf16[96,1536]{1,0:T(8,128)(2,1)S(1)}, bf16[96,1536]{1,0:T(8,128)(2,1)S(1)}, u32[]{:S(2)}, u32[]{:S(2)}) collective-permute-start(bf16[96,1536]{1,0:T(8,128)(2,1)S(1)} %get-tuple-element.203), channel_id=1, source_target_pairs={{1,0},{9,8},{17,16},{25,24},{33,32},{41,40},{49,48},{57,56},{65,64... | collective-permute-start | bytes 884744 | tf_op jit(solution)/shard_map/ppermute | solution.py:564
  179.6 21.1 %collective-permute-start.24 = (bf16[96,1536]{1,0:T(8,128)(2,1)S(1)}, bf16[96,1536]{1,0:T(8,128)(2,1)S(1)}, u32[]{:S(2)}, u32[]{:S(2)}) collective-permute-start(bf16[96,1536]{1,0:T(8,128)(2,1)S(1)} %get-tuple-element.207), channel_id=1, source_target_pairs={{1,0},{9,8},{17,16},{25,24},{33,32},{41,40},{49,48},{57,56},{65,64... | collective-permute-start | bytes 884744 | tf_op jit(solution)/shard_map/ppermute | solution.py:564
  205.6 9.2 %collective-permute-start.25 = (bf16[96,1536]{1,0:T(8,128)(2,1)S(1)}, bf16[96,1536]{1,0:T(8,128)(2,1)S(1)}, u32[]{:S(2)}, u32[]{:S(2)}) collective-permute-start(bf16[96,1536]{1,0:T(8,128)(2,1)S(1)} %get-tuple-element.211), channel_id=1, source_target_pairs={{1,0},{9,8},{17,16},{25,24},{33,32},{41,40},{49,48},{57,56},{65,64... | collective-permute-start | bytes 884744 | tf_op jit(solution)/shard_map/ppermute | solution.py:564
  219.7 7.5 %collective-permute-start.26 = (bf16[96,1536]{1,0:T(8,128)(2,1)S(1)}, bf16[96,1536]{1,0:T(8,128)(2,1)S(1)}, u32[]{:S(2)}, u32[]{:S(2)}) collective-permute-start(bf16[96,1536]{1,0:T(8,128)(2,1)S(1)} %get-tuple-element.215), channel_id=1, source_target_pairs={{1,0},{9,8},{17,16},{25,24},{33,32},{41,40},{49,48},{57,56},{65,64... | collective-permute-start | bytes 884744 | tf_op jit(solution)/shard_map/ppermute | solution.py:564
  243.8 22.1 %collective-permute-start.27 = (bf16[8,2,48,1536]{3,2,1,0:T(8,128)(2,1)S(1)}, bf16[8,2,48,1536]{3,2,1,0:T(8,128)(2,1)S(1)}, u32[]{:S(2)}, u32[]{:S(2)}) collective-permute-start(bf16[8,2,48,1536]{3,2,1,0:T(8,128)(2,1)S(1)} %weight_part.3), channel_id=1, source_target_pairs={{0,8},{8,0},{16,24},{24,16},{32,40},{40,32},{48,56},{56,48},{64,72... | collective-permute-start | bytes 7077896 | tf_op jit(solution)/shard_map/ppermute | solution.py:463
  263.8 2.1 collective-permute-start.28
  266.8 9.2 %collective-permute-start.32 = (bf16[2,56,1536]{2,1,0:T(8,128)(2,1)S(1)}, bf16[2,56,1536]{2,1,0:T(8,128)(2,1)S(1)}, u32[]{:S(2)}, u32[]{:S(2)}) collective-permute-start(bf16[2,56,1536]{2,1,0:T(8,128)(2,1)S(1)} %get-tuple-element.225), channel_id=1, source_target_pairs={{0,128},{8,136},{16,144},{24,152},{32,160},{40,168},{48,176},{56,1... | collective-permute-start | bytes 1032200 | tf_op jit(solution)/shard_map/ppermute | solution.py:466
  266.9 16.5 %collective-permute-start.31 = (bf16[2,56,1536]{2,1,0:T(8,128)(2,1)S(1)}, bf16[2,56,1536]{2,1,0:T(8,128)(2,1)S(1)}, u32[]{:S(2)}, u32[]{:S(2)}) collective-permute-start(bf16[2,56,1536]{2,1,0:T(8,128)(2,1)S(1)} %get-tuple-element.224), channel_id=1, source_target_pairs={{0,128},{8,136},{16,144},{24,152},{32,160},{40,168},{48,176},{56,1... | collective-permute-start | bytes 1032200 | tf_op jit(solution)/shard_map/ppermute | solution.py:466
  276.7 8.3 %collective-permute-start.33 = (bf16[56,1536]{1,0:T(8,128)(2,1)S(1)}, bf16[56,1536]{1,0:T(8,128)(2,1)S(1)}, u32[]{:S(2)}, u32[]{:S(2)}) collective-permute-start(bf16[56,1536]{1,0:T(8,128)(2,1)S(1)} %get-tuple-element.226), channel_id=1, source_target_pairs={{0,16},{8,24},{16,32},{24,40},{32,48},{40,56},{48,64},{56,72},{64,... | collective-permute-start | bytes 516104 | tf_op jit(solution)/shard_map/ppermute | solution.py:460
  278.3 6.7 %collective-permute-start.34 = (bf16[56,1536]{1,0:T(8,128)(2,1)S(1)}, bf16[56,1536]{1,0:T(8,128)(2,1)S(1)}, u32[]{:S(2)}, u32[]{:S(2)}) collective-permute-start(bf16[56,1536]{1,0:T(8,128)(2,1)S(1)} %get-tuple-element.227), channel_id=1, source_target_pairs={{0,112},{8,120},{16,0},{24,8},{32,16},{40,24},{48,32},{56,40},{64,... | collective-permute-start | bytes 516104 | tf_op jit(solution)/shard_map/ppermute | solution.py:460
  282.3 7.8 %collective-permute-start.30 = (bf16[2,56,1536]{2,1,0:T(8,128)(2,1)S(1)}, bf16[2,56,1536]{2,1,0:T(8,128)(2,1)S(1)}, u32[]{:S(2)}, u32[]{:S(2)}) collective-permute-start(bf16[2,56,1536]{2,1,0:T(8,128)(2,1)S(1)} %get-tuple-element.223), channel_id=1, source_target_pairs={{0,128},{8,136},{16,144},{24,152},{32,160},{40,168},{48,176},{56,1... | collective-permute-start | bytes 1032200 | tf_op jit(solution)/shard_map/ppermute | solution.py:466
  285.8 6.7 %collective-permute-start.35 = (bf16[56,1536]{1,0:T(8,128)(2,1)S(1)}, bf16[56,1536]{1,0:T(8,128)(2,1)S(1)}, u32[]{:S(2)}, u32[]{:S(2)}) collective-permute-start(bf16[56,1536]{1,0:T(8,128)(2,1)S(1)} %get-tuple-element.228), channel_id=1, source_target_pairs={{0,16},{8,24},{16,32},{24,40},{32,48},{40,56},{48,64},{56,72},{64,... | collective-permute-start | bytes 516104 | tf_op jit(solution)/shard_map/ppermute | solution.py:460
  285.9 6.6 %collective-permute-start.36 = (bf16[56,1536]{1,0:T(8,128)(2,1)S(1)}, bf16[56,1536]{1,0:T(8,128)(2,1)S(1)}, u32[]{:S(2)}, u32[]{:S(2)}) collective-permute-start(bf16[56,1536]{1,0:T(8,128)(2,1)S(1)} %get-tuple-element.229), channel_id=1, source_target_pairs={{0,112},{8,120},{16,0},{24,8},{32,16},{40,24},{48,32},{56,40},{64,... | collective-permute-start | bytes 516104 | tf_op jit(solution)/shard_map/ppermute | solution.py:460
  289.7 7.4 %collective-permute-start.29 = (bf16[2,56,1536]{2,1,0:T(8,128)(2,1)S(1)}, bf16[2,56,1536]{2,1,0:T(8,128)(2,1)S(1)}, u32[]{:S(2)}, u32[]{:S(2)}) collective-permute-start(bf16[2,56,1536]{2,1,0:T(8,128)(2,1)S(1)} %get-tuple-element.222), channel_id=1, source_target_pairs={{0,128},{8,136},{16,144},{24,152},{32,160},{40,168},{48,176},{56,1... | collective-permute-start | bytes 1032200 | tf_op jit(solution)/shard_map/ppermute | solution.py:466
  293.2 6.6 %collective-permute-start.37 = (bf16[56,1536]{1,0:T(8,128)(2,1)S(1)}, bf16[56,1536]{1,0:T(8,128)(2,1)S(1)}, u32[]{:S(2)}, u32[]{:S(2)}) collective-permute-start(bf16[56,1536]{1,0:T(8,128)(2,1)S(1)} %get-tuple-element.230), channel_id=1, source_target_pairs={{0,16},{8,24},{16,32},{24,40},{32,48},{40,56},{48,64},{56,72},{64,... | collective-permute-start | bytes 516104 | tf_op jit(solution)/shard_map/ppermute | solution.py:460
  294.6 5.3 %collective-permute-start.38 = (bf16[56,1536]{1,0:T(8,128)(2,1)S(1)}, bf16[56,1536]{1,0:T(8,128)(2,1)S(1)}, u32[]{:S(2)}, u32[]{:S(2)}) collective-permute-start(bf16[56,1536]{1,0:T(8,128)(2,1)S(1)} %get-tuple-element.231), channel_id=1, source_target_pairs={{0,112},{8,120},{16,0},{24,8},{32,16},{40,24},{48,32},{56,40},{64,... | collective-permute-start | bytes 516104 | tf_op jit(solution)/shard_map/ppermute | solution.py:460
  300.6 6.6 %collective-permute-start.39 = (bf16[56,1536]{1,0:T(8,128)(2,1)S(1)}, bf16[56,1536]{1,0:T(8,128)(2,1)S(1)}, u32[]{:S(2)}, u32[]{:S(2)}) collective-permute-start(bf16[56,1536]{1,0:T(8,128)(2,1)S(1)} %get-tuple-element.233), channel_id=1, source_target_pairs={{0,16},{8,24},{16,32},{24,40},{32,48},{40,56},{48,64},{56,72},{64,... | collective-permute-start | bytes 516104 | tf_op jit(solution)/shard_map/ppermute | solution.py:460
  307.2 4.6 %collective-permute-start.44 = (bf16[56,1536]{1,0:T(8,128)(2,1)S(1)}, bf16[56,1536]{1,0:T(8,128)(2,1)S(1)}, u32[]{:S(2)}, u32[]{:S(2)}) collective-permute-start(bf16[56,1536]{1,0:T(8,128)(2,1)S(1)} %get-tuple-element.243), channel_id=1, source_target_pairs={{0,112},{8,120},{16,0},{24,8},{32,16},{40,24},{48,32},{56,40},{64,... | collective-permute-start | bytes 516104 | tf_op jit(solution)/shard_map/ppermute | solution.py:460
  309.0 5.5 %collective-permute-start.40 = (bf16[56,1536]{1,0:T(8,128)(2,1)S(1)}, bf16[56,1536]{1,0:T(8,128)(2,1)S(1)}, u32[]{:S(2)}, u32[]{:S(2)}) collective-permute-start(bf16[56,1536]{1,0:T(8,128)(2,1)S(1)} %get-tuple-element.243), channel_id=1, source_target_pairs={{0,16},{8,24},{16,32},{24,40},{32,48},{40,56},{48,64},{56,72},{64,... | collective-permute-start | bytes 516104 | tf_op jit(solution)/shard_map/ppermute | solution.py:460
  314.5 13.6 %collective-permute-start.50 = (bf16[3,56,1536]{2,1,0:T(8,128)(2,1)S(1)}, bf16[3,56,1536]{2,1,0:T(8,128)(2,1)S(1)}, u32[]{:S(2)}, u32[]{:S(2)}) collective-permute-start(bf16[3,56,1536]{2,1,0:T(8,128)(2,1)S(1)} %pad_maximum_fusion.1.rest_0_), channel_id=1, source_target_pairs={{0,128},{8,136},{16,144},{24,152},{32,160},{40,168},{48,176},{56,1... | collective-permute-start | bytes 1548296 | tf_op jit(solution)/shard_map/ppermute | solution.py:466
  314.9 4.6 %collective-permute-start.45 = (bf16[56,1536]{1,0:T(8,128)(2,1)S(1)}, bf16[56,1536]{1,0:T(8,128)(2,1)S(1)}, u32[]{:S(2)}, u32[]{:S(2)}) collective-permute-start(bf16[56,1536]{1,0:T(8,128)(2,1)S(1)} %collective-permute-done.44), channel_id=1, source_target_pairs={{0,112},{8,120},{16,0},{24,8},{32,16},{40,24},{48,32},{56,40},{64,... | collective-permute-start | bytes 516104 | tf_op jit(solution)/shard_map/ppermute | solution.py:460
  314.9 5.8 %collective-permute-start.41 = (bf16[56,1536]{1,0:T(8,128)(2,1)S(1)}, bf16[56,1536]{1,0:T(8,128)(2,1)S(1)}, u32[]{:S(2)}, u32[]{:S(2)}) collective-permute-start(bf16[56,1536]{1,0:T(8,128)(2,1)S(1)} %collective-permute-done.40), channel_id=1, source_target_pairs={{0,16},{8,24},{16,32},{24,40},{32,48},{40,56},{48,64},{56,72},{64,... | collective-permute-start | bytes 516104 | tf_op jit(solution)/shard_map/ppermute | solution.py:460
  320.8 10.1 %collective-permute-start.51 = (bf16[2,56,1536]{2,1,0:T(8,128)(2,1)S(1)}, bf16[2,56,1536]{2,1,0:T(8,128)(2,1)S(1)}, u32[]{:S(2)}, u32[]{:S(2)}) collective-permute-start(bf16[2,56,1536]{2,1,0:T(8,128)(2,1)S(1)} %pad_maximum_fusion.3.rest_2_), channel_id=1, source_target_pairs={{0,128},{8,136},{16,144},{24,152},{32,160},{40,168},{48,176},{56,1... | collective-permute-start | bytes 1032200 | tf_op jit(solution)/shard_map/ppermute | solution.py:466
  321.7 6.4 %collective-permute-start.46 = (bf16[56,1536]{1,0:T(8,128)(2,1)S(1)}, bf16[56,1536]{1,0:T(8,128)(2,1)S(1)}, u32[]{:S(2)}, u32[]{:S(2)}) collective-permute-start(bf16[56,1536]{1,0:T(8,128)(2,1)S(1)} %collective-permute-done.45), channel_id=1, source_target_pairs={{0,112},{8,120},{16,0},{24,8},{32,16},{40,24},{48,32},{56,40},{64,... | collective-permute-start | bytes 516104 | tf_op jit(solution)/shard_map/ppermute | solution.py:460
  321.7 6.4 %collective-permute-start.42 = (bf16[56,1536]{1,0:T(8,128)(2,1)S(1)}, bf16[56,1536]{1,0:T(8,128)(2,1)S(1)}, u32[]{:S(2)}, u32[]{:S(2)}) collective-permute-start(bf16[56,1536]{1,0:T(8,128)(2,1)S(1)} %collective-permute-done.41), channel_id=1, source_target_pairs={{0,16},{8,24},{16,32},{24,40},{32,48},{40,56},{48,64},{56,72},{64,... | collective-permute-start | bytes 516104 | tf_op jit(solution)/shard_map/ppermute | solution.py:460
  330.9 22.7 %collective-permute-start.52 = (bf16[12,56,1536]{2,1,0:T(8,128)(2,1)S(1)}, bf16[12,56,1536]{2,1,0:T(8,128)(2,1)S(1)}, u32[]{:S(2)}, u32[]{:S(2)}) collective-permute-start(bf16[12,56,1536]{2,1,0:T(8,128)(2,1)S(1)} %constant_dynamic-update-slice_fusion), channel_id=1, source_target_pairs={{0,8},{8,0},{16,24},{24,16},{32,40},{40,32},{48,56},{56,48},{64,72... | collective-permute-start | bytes 6193160 | tf_op jit(solution)/shard_map/ppermute | solution.py:463
  339.1 7.1 %collective-permute-start.43 = (bf16[56,1536]{1,0:T(8,128)(2,1)S(1)}, bf16[56,1536]{1,0:T(8,128)(2,1)S(1)}, u32[]{:S(2)}, u32[]{:S(2)}) collective-permute-start(bf16[56,1536]{1,0:T(8,128)(2,1)S(1)} %collective-permute-done.42), channel_id=1, source_target_pairs={{0,16},{8,24},{16,32},{24,40},{32,48},{40,56},{48,64},{56,72},{64,... | collective-permute-start | bytes 516104 | tf_op jit(solution)/shard_map/ppermute | solution.py:460
  339.1 12.9 %collective-permute-start.47 = (bf16[2,56,1536]{2,1,0:T(8,128)(2,1)S(1)}, bf16[2,56,1536]{2,1,0:T(8,128)(2,1)S(1)}, u32[]{:S(2)}, u32[]{:S(2)}) collective-permute-start(bf16[2,56,1536]{2,1,0:T(8,128)(2,1)S(1)} %pad_maximum_fusion.2.rest_3_), channel_id=1, source_target_pairs={{0,128},{8,136},{16,144},{24,152},{32,160},{40,168},{48,176},{56,1... | collective-permute-start | bytes 1032200 | tf_op jit(solution)/shard_map/ppermute | solution.py:466
  346.2 5.8 %collective-permute-start.48 = (bf16[1,56,1536]{2,1,0:T(8,128)(2,1)S(1)}, bf16[1,56,1536]{2,1,0:T(8,128)(2,1)S(1)}, u32[]{:S(2)}, u32[]{:S(2)}) collective-permute-start(bf16[1,56,1536]{2,1,0:T(8,128)(2,1)S(1)} %bitcast.71), channel_id=1, source_target_pairs={{0,128},{8,136},{16,144},{24,152},{32,160},{40,168},{48,176},{56,1... | collective-permute-start | bytes 516104 | tf_op jit(solution)/shard_map/ppermute | solution.py:466
  352.1 4.0 %collective-permute-start.49 = (bf16[4,56,1536]{2,1,0:T(8,128)(2,1)S(1)}, bf16[4,56,1536]{2,1,0:T(8,128)(2,1)S(1)}, u32[]{:S(2)}, u32[]{:S(2)}) collective-permute-start(bf16[4,56,1536]{2,1,0:T(8,128)(2,1)S(1)} %pad_maximum_fusion), channel_id=1, source_target_pairs={{0,8},{8,0},{16,24},{24,16},{32,40},{40,32},{48,56},{56,48},{64,72... | collective-permute-start | bytes 2064392 | tf_op jit(solution)/shard_map/ppermute | solution.py:463

commit v2 on v1

--- a/solution.py
+++ b/solution.py
@@ -23,7 +23,7 @@
             j = 8 * high + low - 1
             if 0 <= j < TAPS:
                 row = TAPS - 1 - j if reverse else j
-                term = taps[0, row : row + 1, cols] * shifted[8 * high : 8 * high + FRAMES]
+                term = taps[row, :, cols] * shifted[8 * high : 8 * high + FRAMES]
                 total = term if total is None else total + term
     return total
 
@@ -231,19 +231,22 @@
             return carry
 
         lax.fori_loop(0, chunks, one_chunk, 0)
-        mean_row = jnp.sum(mean_sum[...], axis=1, keepdims=True) * (1.0 / width)
-        dot_row = jnp.sum(dot_sum[...], axis=1, keepdims=True) * (1.0 / width)
-        mean_row = jnp.broadcast_to(mean_row, (FRAMES, LANES))
-        dot_row = jnp.broadcast_to(dot_row, (FRAMES, LANES))
-        inv_std = inv_all[slot]
-
-        def finish(tile, carry):
-            cols = lane_tile(tile)
-            change = inv_std * (scaled_now[:, cols] - mean_row - norm_all[slot, :, cols] * dot_row)
-            out[:, cols] = (grad_out[:, cols].astype(jnp.float32) + change).astype(jnp.bfloat16)
-            return carry
-
-        lax.fori_loop(0, tiles, finish, 0, unroll=2)
+
+        @pl.when(section != 0)
+        def _():
+            mean_row = jnp.sum(mean_sum[...], axis=1, keepdims=True) * (1.0 / width)
+            dot_row = jnp.sum(dot_sum[...], axis=1, keepdims=True) * (1.0 / width)
+            mean_row = jnp.broadcast_to(mean_row, (FRAMES, LANES))
+            dot_row = jnp.broadcast_to(dot_row, (FRAMES, LANES))
+            inv_std = inv_all[slot]
+
+            def finish(tile, carry):
+                cols = lane_tile(tile)
+                change = inv_std * (scaled_now[:, cols] - mean_row - norm_all[slot, :, cols] * dot_row)
+                out[:, cols] = (grad_out[:, cols].astype(jnp.float32) + change).astype(jnp.bfloat16)
+                return carry
+
+            lax.fori_loop(0, tiles, finish, 0, unroll=2)
 
 
 def backward_call(tick, sections, info, seeds, recv, crossed, weight, taps, gain, stash, held):
@@ -315,7 +318,7 @@
         lax.fori_loop(0, width // LANES, one_tile, 0)
 
 
-def on_chip(kernel, name, shapes, operands, scratch=(), aliases=None, hbm_out=()):
+def on_chip(kernel, name, shapes, operands, scratch=(), aliases=None, hbm_out=(), flops=10**6):
     vmem = pl.BlockSpec(memory_space=pltpu.VMEM)
     smem = pl.BlockSpec(memory_space=pltpu.SMEM)
     anywhere = pl.BlockSpec(memory_space=pl.ANY)
@@ -329,7 +332,7 @@
         scratch_shapes=list(scratch),
         input_output_aliases=aliases,
         compiler_params=pltpu.CompilerParams(vmem_limit_bytes=VMEM),
-        cost_estimate=pl.CostEstimate(flops=10**6, bytes_accessed=2**10, transcendentals=0),
+        cost_estimate=pl.CostEstimate(flops=flops, bytes_accessed=2**10, transcendentals=0),
         name=name,
     )(*operands)
 
@@ -418,7 +421,7 @@
     if last:
         taps_out, gain_out = rest[-3:-1]
         for row in range(TAPS):
-            taps_out[0, row : row + 1, :] = edge[row, 0:1, :]
+            taps_out[row] = edge[row, 0:1, :]
         gain_out[...] = edge[TAPS, 0:1, :]
     for copy in copies:
         copy.wait()
@@ -437,11 +440,12 @@
         functools.partial(place_kernel, ring, sources, count, held is not None),
         "place_sums",
         [(shape, jnp.bfloat16), ((4 * ring, EXTRA, shape[1]), jnp.float32)]
-        + ([((1, TAPS, shape[1]), jnp.float32), ((1, shape[1]), jnp.float32)] if held else []),
+        + ([((TAPS, 1, shape[1]), jnp.float32), ((1, shape[1]), jnp.float32)] if held else []),
         (info, *blocks, *(held or ())),
         [pltpu.SemaphoreType.DMA((len(sources),))],
         {count + 1: 0, count + 2: 1} if held else {},
         hbm_out=(0,),
+        flops=10**6 if held else 5 * 10**9,
     )
 
 
@@ -539,7 +543,7 @@
 
 def body(mels, lengths, sub_weight, block_weight, conv_kernel, norm_gain, cotangent):
     weight = block_weight[0]
-    taps = conv_kernel
+    taps = jnp.transpose(conv_kernel, (1, 0, 2))
     gain = norm_gain
     width = cotangent.shape[1]
     groups = lengths.shape[0]
@@ -623,7 +627,7 @@
         return taps_call(ticks, sections, info, held, stash, gain, sums)
 
     weight_sum, taps_sums, gain_sum = column_sum(info, stash[3], held[0], last_sums, shards)
-    return (weight_sum[None], taps_sums, gain_sum)
+    return (weight_sum[None], jnp.transpose(taps_sums, (1, 0, 2)), gain_sum)
 
 
 def solution(mesh):

time: 364 us -> 361 us (level)
  transfers between devices with their start and end apart: 53 -> 53, of which waited for: 22 -> 22; matrix products, arithmetic and copies ran while one was open for 1% -> 0% of each run, Pallas kernels for 7% -> 8%
where the time goes in v2:
time: 361 us; the launch traced here: 357 us
  waiting for transfers between devices  194 us (54%)
  starting transfers between devices  81.2 us (22%)
  Pallas kernels  75.1 us (21%)
    ppermute x25, waiting for transfers between devices, relay(): return lax.ppermute(block, ('dp', 'section'), route)  143 us
    ppermute x14, waiting for transfers between devices, along_z(): return lax.ppermute(block, 'dp', route)  33.5 us
    pallas_call x12, Pallas kernels, backward_call(): pl.pallas_call(functools.partial(backward_kernel, tick, sections), out_sh...  32.9 us
    ppermute x25, starting transfers between devices, relay(): return lax.ppermute(block, ('dp', 'section'), route)  29.6 us
    ppermute x4, starting transfers between devices, to_core(): return lax.ppermute(block, 'dp', [(d, d ^ 1) for d in range(shards)])  27.2 us
    pallas_call x17, Pallas kernels, on_chip(): pl.pallas_call(kernel, out_shape=tuple((jax.ShapeDtypeStruct(shape, dtype...  24 us
    ppermute x14, starting transfers between devices, along_z(): return lax.ppermute(block, 'dp', route)  19.1 us
    pallas_call x11, Pallas kernels, forward_call(): pl.pallas_call(functools.partial(forward_kernel, tick, sections), out_sha...  18.2 us
  transfers between devices with their start and end apart: 53, of which 22 were waited for; matrix products, arithmetic and copies ran while one was open for 0% of the time, Pallas kernels for 8%

profile of v2, /device:TPU:1, one launch (start us, length us, event | category | flops | bytes accessed | tf_op | source)
XLA Modules:
  0.0 356.6 jit_solution(1942848786638617248)
XLA Ops:
  1.5 1.0 reshape.19
  3.2 2.3 copy-done.1
  5.5 3.5 section_forward.11
  9.0 1.4 collective-permute-start.1
  10.4 3.6 %collective-permute-done.1.recv = bf16[96,1536]{1,0:T(8,128)(2,1)S(1)} collective-permute-done((bf16[96,1536]{1,0:T(8,128)(2,1)S(1)}, bf16[96,1536]{1,0:T(8,128)(2,1)S(1)}, u32[]{:S(2)}, u32[]{:S(2)}) %collective-permute-start.1) | collective-permute-done | bytes 294944 | tf_op jit(solution)/shard_map/ppermute | solution.py:568
  14.0 3.4 section_forward.12
  17.4 3.8 %collective-permute-start.2 = (bf16[96,1536]{1,0:T(8,128)(2,1)S(1)}, bf16[96,1536]{1,0:T(8,128)(2,1)S(1)}, u32[]{:S(2)}, u32[]{:S(2)}) collective-permute-start(bf16[96,1536]{1,0:T(8,128)(2,1)S(1)} %get-tuple-element.126), channel_id=1, source_target_pairs={{0,1},{8,9},{16,17},{24,25},{32,33},{40,41},{48,49},{56,57},{64,65... | collective-permute-start | bytes 884744 | tf_op jit(solution)/shard_map/ppermute | solution.py:568
  21.3 3.6 %collective-permute-done.2.recv = bf16[96,1536]{1,0:T(8,128)(2,1)S(1)} collective-permute-done((bf16[96,1536]{1,0:T(8,128)(2,1)S(1)}, bf16[96,1536]{1,0:T(8,128)(2,1)S(1)}, u32[]{:S(2)}, u32[]{:S(2)}) %collective-permute-start.2) | collective-permute-done | bytes 294944 | tf_op jit(solution)/shard_map/ppermute | solution.py:568
  24.9 3.4 section_forward.13
  28.3 3.8 %collective-permute-start.3 = (bf16[96,1536]{1,0:T(8,128)(2,1)S(1)}, bf16[96,1536]{1,0:T(8,128)(2,1)S(1)}, u32[]{:S(2)}, u32[]{:S(2)}) collective-permute-start(bf16[96,1536]{1,0:T(8,128)(2,1)S(1)} %get-tuple-element.131), channel_id=1, source_target_pairs={{0,1},{8,9},{16,17},{24,25},{32,33},{40,41},{48,49},{56,57},{64,65... | collective-permute-start | bytes 884744 | tf_op jit(solution)/shard_map/ppermute | solution.py:568
  32.1 3.6 %collective-permute-done.3.recv = bf16[96,1536]{1,0:T(8,128)(2,1)S(1)} collective-permute-done((bf16[96,1536]{1,0:T(8,128)(2,1)S(1)}, bf16[96,1536]{1,0:T(8,128)(2,1)S(1)}, u32[]{:S(2)}, u32[]{:S(2)}) %collective-permute-start.3) | collective-permute-done | bytes 294944 | tf_op jit(solution)/shard_map/ppermute | solution.py:568
  35.7 3.4 section_forward.14
  39.1 3.8 %collective-permute-start.4 = (bf16[96,1536]{1,0:T(8,128)(2,1)S(1)}, bf16[96,1536]{1,0:T(8,128)(2,1)S(1)}, u32[]{:S(2)}, u32[]{:S(2)}) collective-permute-start(bf16[96,1536]{1,0:T(8,128)(2,1)S(1)} %get-tuple-element.136), channel_id=1, source_target_pairs={{0,1},{8,9},{16,17},{24,25},{32,33},{40,41},{48,49},{56,57},{64,65... | collective-permute-start | bytes 884744 | tf_op jit(solution)/shard_map/ppermute | solution.py:568
  43.7 2.9 collective-permute-done.4.recv
  58.2 1.3 section_forward.21
  69.5 1.3 collective-permute-start.22
  71.4 102.3 %collective-permute-done.22.recv = bf16[96,1536]{1,0:T(8,128)(2,1)S(1)} collective-permute-done((bf16[96,1536]{1,0:T(8,128)(2,1)S(1)}, bf16[96,1536]{1,0:T(8,128)(2,1)S(1)}, u32[]{:S(2)}, u32[]{:S(2)}) %collective-permute-start.22) | collective-permute-done | bytes 294944 | tf_op jit(solution)/shard_map/ppermute | solution.py:568
  173.7 4.6 %section_backward.20 = (bf16[96,1536]{1,0:T(8,128)(2,1)S(1)}, bf16[4,96,1536]{2,1,0:T(8,128)(2,1)S(1)}, f32[4,96,1536]{2,1,0:T(8,128)S(1)}, f32[4,8,1536]{2,1,0:T(8,128)S(1)}) custom-call(s32[8]{0:T(128)S(1)} %concatenate.10.info, bf16[4,96,1536]{2,1,0:T(8,128)(2,1)S(1)} %bitcast.58, ...), custom_call_target="tpu_custom_call", output_to_operand_aliasing={{1}: (10, {}), {2}: (11, {}), {3}: (12, {})} | custom-call | flops 1000000 | bytes 1024 | tf_op jit(solution)/shard_map/section_backward/pallas_call | solution.py:264
  178.3 1.3 collective-permute-start.24
  179.6 2.3 taps_gradient.12.rest_0_
  181.9 18.1 %collective-permute-done.24.recv = bf16[96,1536]{1,0:T(8,128)(2,1)S(1)} collective-permute-done((bf16[96,1536]{1,0:T(8,128)(2,1)S(1)}, bf16[96,1536]{1,0:T(8,128)(2,1)S(1)}, u32[]{:S(2)}, u32[]{:S(2)}) %collective-permute-start.24) | collective-permute-done | bytes 294944 | tf_op jit(solution)/shard_map/ppermute | solution.py:568
  200.0 4.6 %section_backward.21 = (bf16[96,1536]{1,0:T(8,128)(2,1)S(1)}, bf16[4,96,1536]{2,1,0:T(8,128)(2,1)S(1)}, f32[4,96,1536]{2,1,0:T(8,128)S(1)}, f32[4,8,1536]{2,1,0:T(8,128)S(1)}) custom-call(s32[8]{0:T(128)S(1)} %concatenate.10.info, bf16[4,96,1536]{2,1,0:T(8,128)(2,1)S(1)} %bitcast.59, ...), custom_call_target="tpu_custom_call", output_to_operand_aliasing={{1}: (10, {}), {2}: (11, {}), {3}: (12, {})} | custom-call | flops 1000000 | bytes 1024 | tf_op jit(solution)/shard_map/section_backward/pallas_call | solution.py:264
  204.7 1.3 collective-permute-start.25
  206.0 2.3 taps_gradient.13.rest_0_
  208.3 5.4 %collective-permute-done.25.recv = bf16[96,1536]{1,0:T(8,128)(2,1)S(1)} collective-permute-done((bf16[96,1536]{1,0:T(8,128)(2,1)S(1)}, bf16[96,1536]{1,0:T(8,128)(2,1)S(1)}, u32[]{:S(2)}, u32[]{:S(2)}) %collective-permute-start.25) | collective-permute-done | bytes 294944 | tf_op jit(solution)/shard_map/ppermute | solution.py:568
  213.7 4.6 %section_backward.22 = (bf16[96,1536]{1,0:T(8,128)(2,1)S(1)}, bf16[4,96,1536]{2,1,0:T(8,128)(2,1)S(1)}, f32[4,96,1536]{2,1,0:T(8,128)S(1)}, f32[4,8,1536]{2,1,0:T(8,128)S(1)}) custom-call(s32[8]{0:T(128)S(1)} %concatenate.10.info, bf16[4,96,1536]{2,1,0:T(8,128)(2,1)S(1)} %bitcast.60, ...), custom_call_target="tpu_custom_call", output_to_operand_aliasing={{1}: (10, {}), {2}: (11, {}), {3}: (12, {})} | custom-call | flops 1000000 | bytes 1024 | tf_op jit(solution)/shard_map/section_backward/pallas_call | solution.py:264
  218.3 1.3 collective-permute-start.26
  219.6 2.3 taps_gradient.14.rest_0_
  222.0 3.8 %collective-permute-done.26.recv = bf16[96,1536]{1,0:T(8,128)(2,1)S(1)} collective-permute-done((bf16[96,1536]{1,0:T(8,128)(2,1)S(1)}, bf16[96,1536]{1,0:T(8,128)(2,1)S(1)}, u32[]{:S(2)}, u32[]{:S(2)}) %collective-permute-start.26) | collective-permute-done | bytes 294944 | tf_op jit(solution)/shard_map/ppermute | solution.py:568
  225.8 14.3 %section_backward.23 = (bf16[96,1536]{1,0:T(8,128)(2,1)}, bf16[4,96,1536]{2,1,0:T(8,128)(2,1)S(1)}, f32[4,96,1536]{2,1,0:T(8,128)S(1)}, f32[4,8,1536]{2,1,0:T(8,128)S(1)}) custom-call(s32[8]{0:T(128)S(1)} %concatenate.10.info, bf16[4,96,1536]{2,1,0:T(8,128)(2,1)S(1)} %bitcast.61, ...), custom_call_target="tpu_custom_call", output_to_operand_aliasing={{1}: (10, {}), {2}: (11, {}), {3}: (12, {})} | custom-call | flops 1000000 | bytes 1024 | tf_op jit(solution)/shard_map/section_backward/pallas_call | solution.py:264
  240.1 2.0 weight_part.3
  242.1 17.5 %collective-permute-start.27 = (bf16[8,2,48,1536]{3,2,1,0:T(8,128)(2,1)S(1)}, bf16[8,2,48,1536]{3,2,1,0:T(8,128)(2,1)S(1)}, u32[]{:S(2)}, u32[]{:S(2)}) collective-permute-start(bf16[8,2,48,1536]{3,2,1,0:T(8,128)(2,1)S(1)} %weight_part.3), channel_id=1, source_target_pairs={{0,8},{8,0},{16,24},{24,16},{32,40},{40,32},{48,56},{56,48},{64,72... | collective-permute-start | bytes 7077896 | tf_op jit(solution)/shard_map/ppermute | solution.py:467
  259.6 2.3 taps_gradient.15.sums
  262.0 2.0 weight_part.2.mine
  264.0 0.9 ring_step.5
  265.0 1.5 collective-permute-start.31
  266.5 7.7 %collective-permute-done.32.rest_0_ = bf16[2,56,1536]{2,1,0:T(8,128)(2,1)S(1)} collective-permute-done((bf16[2,56,1536]{2,1,0:T(8,128)(2,1)S(1)}, bf16[2,56,1536]{2,1,0:T(8,128)(2,1)S(1)}, u32[]{:S(2)}, u32[]{:S(2)}) %collective-permute-start.32) | collective-permute-done | bytes 344096 | tf_op jit(solution)/shard_map/ppermute | solution.py:470
  274.8 1.3 collective-permute-start.33
  276.2 4.0 %collective-permute-start.34 = (bf16[56,1536]{1,0:T(8,128)(2,1)S(1)}, bf16[56,1536]{1,0:T(8,128)(2,1)S(1)}, u32[]{:S(2)}, u32[]{:S(2)}) collective-permute-start(bf16[56,1536]{1,0:T(8,128)(2,1)S(1)} %get-tuple-element.227), channel_id=1, source_target_pairs={{0,112},{8,120},{16,0},{24,8},{32,16},{40,24},{48,32},{56,40},{64,... | collective-permute-start | bytes 516104 | tf_op jit(solution)/shard_map/ppermute | solution.py:464
  280.5 1.0 collective-permute-done.31.rest_0_
  281.5 1.4 collective-permute-done.33.rest_1_
  283.7 3.9 %collective-permute-start.36 = (bf16[56,1536]{1,0:T(8,128)(2,1)S(1)}, bf16[56,1536]{1,0:T(8,128)(2,1)S(1)}, u32[]{:S(2)}, u32[]{:S(2)}) collective-permute-start(bf16[56,1536]{1,0:T(8,128)(2,1)S(1)} %get-tuple-element.229), channel_id=1, source_target_pairs={{0,112},{8,120},{16,0},{24,8},{32,16},{40,24},{48,32},{56,40},{64,... | collective-permute-start | bytes 516104 | tf_op jit(solution)/shard_map/ppermute | solution.py:464
  287.9 2.4 collective-permute-done.35.rest_1_
  291.1 1.4 collective-permute-start.37
  292.5 2.5 collective-permute-start.38
  295.0 2.7 collective-permute-done.37.rest_1_
  298.4 1.2 collective-permute-start.39
  299.6 5.5 %collective-permute-done.39 = bf16[56,1536]{1,0:T(8,128)(2,1)S(1)} collective-permute-done((bf16[56,1536]{1,0:T(8,128)(2,1)S(1)}, bf16[56,1536]{1,0:T(8,128)(2,1)S(1)}, u32[]{:S(2)}, u32[]{:S(2)}) %collective-permute-start.39) | collective-permute-done | bytes 172064 | tf_op jit(solution)/shard_map/ppermute | solution.py:464
  305.1 1.7 collective-permute-start.44
  306.9 2.8 collective-permute-done.44
  309.7 2.6 collective-permute-done.40
  312.8 1.5 collective-permute-start.41
  314.3 3.0 collective-permute-done.45
  317.3 1.3 collective-permute-done.41
  318.7 0.8 collective-permute-start.51
  319.5 1.5 collective-permute-start.42
  321.0 4.9 %collective-permute-done.42 = bf16[56,1536]{1,0:T(8,128)(2,1)S(1)} collective-permute-done((bf16[56,1536]{1,0:T(8,128)(2,1)S(1)}, bf16[56,1536]{1,0:T(8,128)(2,1)S(1)}, u32[]{:S(2)}, u32[]{:S(2)}) %collective-permute-start.42) | collective-permute-done | bytes 172064 | tf_op jit(solution)/shard_map/ppermute | solution.py:464
  326.0 2.8 collective-permute-done.51.rest_5_
  328.9 8.1 %collective-permute-start.52 = (bf16[12,56,1536]{2,1,0:T(8,128)(2,1)S(1)}, bf16[12,56,1536]{2,1,0:T(8,128)(2,1)S(1)}, u32[]{:S(2)}, u32[]{:S(2)}) collective-permute-start(bf16[12,56,1536]{2,1,0:T(8,128)(2,1)S(1)} %constant_dynamic-update-slice_fusion), channel_id=1, source_target_pairs={{0,8},{8,0},{16,24},{24,16},{32,40},{40,32},{48,56},{56,48},{64,72... | collective-permute-start | bytes 6193160 | tf_op jit(solution)/shard_map/ppermute | solution.py:467
  337.2 6.9 %collective-permute-done.43 = bf16[56,1536]{1,0:T(8,128)(2,1)S(1)} collective-permute-done((bf16[56,1536]{1,0:T(8,128)(2,1)S(1)}, bf16[56,1536]{1,0:T(8,128)(2,1)S(1)}, u32[]{:S(2)}, u32[]{:S(2)}) %collective-permute-start.43) | collective-permute-done | bytes 172064 | tf_op jit(solution)/shard_map/ppermute | solution.py:464
  344.2 5.7 %collective-permute-done.48.rest_3_ = bf16[1,56,1536]{2,1,0:T(8,128)(2,1)S(1)} collective-permute-done((bf16[1,56,1536]{2,1,0:T(8,128)(2,1)S(1)}, bf16[1,56,1536]{2,1,0:T(8,128)(2,1)S(1)}, u32[]{:S(2)}, u32[]{:S(2)}) %collective-permute-start.48) | collective-permute-done | bytes 172064 | tf_op jit(solution)/shard_map/ppermute | solution.py:470
  350.0 1.5 collective-permute-start.49
  351.4 2.5 place_sums.2
  354.0 2.3 place_sums.3
  (114 shorter events, 29.0 us)
Async XLA Ops:
  0.6 1.9 copy-start
  0.6 2.4 copy-start.5
  0.7 2.5 copy-start.4
  0.7 2.5 copy-start.3
  0.7 2.4 collective-permute-start
  3.2 2.3 copy-start.1
  5.5 8.5 %copy-start.2 = (bf16[1,1536,1536]{2,1,0:T(8,128)(2,1)S(1)}, bf16[1,1536,1536]{2,1,0:T(8,128)(2,1)}, u32[]{:S(2)}) copy-start(bf16[1,1536,1536]{2,1,0:T(8,128)(2,1)} %param.10) | copy-start | bytes 14155780
  9.0 5.0 %collective-permute-start.1 = (bf16[96,1536]{1,0:T(8,128)(2,1)S(1)}, bf16[96,1536]{1,0:T(8,128)(2,1)S(1)}, u32[]{:S(2)}, u32[]{:S(2)}) collective-permute-start(bf16[96,1536]{1,0:T(8,128)(2,1)S(1)} %get-tuple-element.121), channel_id=1, source_target_pairs={{0,1},{8,9},{16,17},{24,25},{32,33},{40,41},{48,49},{56,57},{64,65... | collective-permute-start | bytes 884744 | tf_op jit(solution)/shard_map/ppermute | solution.py:568
  17.4 7.5 %collective-permute-start.2 = (bf16[96,1536]{1,0:T(8,128)(2,1)S(1)}, bf16[96,1536]{1,0:T(8,128)(2,1)S(1)}, u32[]{:S(2)}, u32[]{:S(2)}) collective-permute-start(bf16[96,1536]{1,0:T(8,128)(2,1)S(1)} %get-tuple-element.126), channel_id=1, source_target_pairs={{0,1},{8,9},{16,17},{24,25},{32,33},{40,41},{48,49},{56,57},{64,65... | collective-permute-start | bytes 884744 | tf_op jit(solution)/shard_map/ppermute | solution.py:568
  28.3 7.5 %collective-permute-start.3 = (bf16[96,1536]{1,0:T(8,128)(2,1)S(1)}, bf16[96,1536]{1,0:T(8,128)(2,1)S(1)}, u32[]{:S(2)}, u32[]{:S(2)}) collective-permute-start(bf16[96,1536]{1,0:T(8,128)(2,1)S(1)} %get-tuple-element.131), channel_id=1, source_target_pairs={{0,1},{8,9},{16,17},{24,25},{32,33},{40,41},{48,49},{56,57},{64,65... | collective-permute-start | bytes 884744 | tf_op jit(solution)/shard_map/ppermute | solution.py:568
  35.7 7.2 %copy-start.6 = (bf16[384,1536]{1,0:T(8,128)(2,1)S(1)}, bf16[384,1536]{1,0:T(8,128)(2,1)}, u32[]{:S(2)}) copy-start(bf16[384,1536]{1,0:T(8,128)(2,1)} %param.13) | copy-start | bytes 3538948
  39.1 7.5 %collective-permute-start.4 = (bf16[96,1536]{1,0:T(8,128)(2,1)S(1)}, bf16[96,1536]{1,0:T(8,128)(2,1)S(1)}, u32[]{:S(2)}, u32[]{:S(2)}) collective-permute-start(bf16[96,1536]{1,0:T(8,128)(2,1)S(1)} %get-tuple-element.136), channel_id=1, source_target_pairs={{0,1},{8,9},{16,17},{24,25},{32,33},{40,41},{48,49},{56,57},{64,65... | collective-permute-start | bytes 884744 | tf_op jit(solution)/shard_map/ppermute | solution.py:568
  43.0 8.6 %collective-permute-start.11 = (bf16[384,1536]{1,0:T(8,128)(2,1)S(1)}, bf16[384,1536]{1,0:T(8,128)(2,1)S(1)}, u32[]{:S(2)}, u32[]{:S(2)}) collective-permute-start(bf16[384,1536]{1,0:T(8,128)(2,1)S(1)} %copy-done.6), channel_id=1, source_target_pairs={{7,135},{15,143},{23,151},{31,159},{39,167},{47,175},{55,183},{63,... | collective-permute-start | bytes 3538952 | tf_op jit(solution)/shard_map/ppermute | solution.py:577
  47.1 0.7 collective-permute-start.5
  48.4 0.7 collective-permute-start.6
  49.7 0.7 collective-permute-start.7
  50.9 2.0 collective-permute-start.8
  52.2 1.9 collective-permute-start.12
  53.4 2.2 collective-permute-start.9
  55.0 1.9 collective-permute-start.13
  56.2 2.0 collective-permute-start.10
  57.5 2.0 collective-permute-start.14
  60.0 1.4 collective-permute-start.15
  60.7 3.2 collective-permute-start.17
  62.0 2.0 collective-permute-start.16
  62.7 3.8 %collective-permute-start.19 = (bf16[96,1536]{1,0:T(8,128)(2,1)S(1)}, bf16[96,1536]{1,0:T(8,128)(2,1)S(1)}, u32[]{:S(2)}, u32[]{:S(2)}) collective-permute-start(bf16[96,1536]{1,0:T(8,128)(2,1)S(1)} %get-tuple-element.191), channel_id=1, source_target_pairs={{4,131},{12,139},{20,147},{28,155},{36,163},{44,171},{52,179},{60,... | collective-permute-start | bytes 884744 | tf_op jit(solution)/shard_map/ppermute | solution.py:568
  64.5 1.9 collective-permute-start.18
  65.2 3.8 %collective-permute-start.21 = (bf16[96,1536]{1,0:T(8,128)(2,1)S(1)}, bf16[96,1536]{1,0:T(8,128)(2,1)S(1)}, u32[]{:S(2)}, u32[]{:S(2)}) collective-permute-start(bf16[96,1536]{1,0:T(8,128)(2,1)S(1)} %get-tuple-element.195), channel_id=1, source_target_pairs={{4,131},{12,139},{20,147},{28,155},{36,163},{44,171},{52,179},{60,... | collective-permute-start | bytes 884744 | tf_op jit(solution)/shard_map/ppermute | solution.py:568
  67.0 1.9 collective-permute-start.20
  67.7 3.7 %collective-permute-start.23 = (bf16[96,1536]{1,0:T(8,128)(2,1)S(1)}, bf16[96,1536]{1,0:T(8,128)(2,1)S(1)}, u32[]{:S(2)}, u32[]{:S(2)}) collective-permute-start(bf16[96,1536]{1,0:T(8,128)(2,1)S(1)} %get-tuple-element.199), channel_id=1, source_target_pairs={{4,131},{12,139},{20,147},{28,155},{36,163},{44,171},{52,179},{60,... | collective-permute-start | bytes 884744 | tf_op jit(solution)/shard_map/ppermute | solution.py:568
  69.5 104.1 %collective-permute-start.22 = (bf16[96,1536]{1,0:T(8,128)(2,1)S(1)}, bf16[96,1536]{1,0:T(8,128)(2,1)S(1)}, u32[]{:S(2)}, u32[]{:S(2)}) collective-permute-start(bf16[96,1536]{1,0:T(8,128)(2,1)S(1)} %get-tuple-element.203), channel_id=1, source_target_pairs={{1,0},{9,8},{17,16},{25,24},{33,32},{41,40},{49,48},{57,56},{65,64... | collective-permute-start | bytes 884744 | tf_op jit(solution)/shard_map/ppermute | solution.py:568
  178.3 21.7 %collective-permute-start.24 = (bf16[96,1536]{1,0:T(8,128)(2,1)S(1)}, bf16[96,1536]{1,0:T(8,128)(2,1)S(1)}, u32[]{:S(2)}, u32[]{:S(2)}) collective-permute-start(bf16[96,1536]{1,0:T(8,128)(2,1)S(1)} %get-tuple-element.207), channel_id=1, source_target_pairs={{1,0},{9,8},{17,16},{25,24},{33,32},{41,40},{49,48},{57,56},{65,64... | collective-permute-start | bytes 884744 | tf_op jit(solution)/shard_map/ppermute | solution.py:568
  204.7 9.0 %collective-permute-start.25 = (bf16[96,1536]{1,0:T(8,128)(2,1)S(1)}, bf16[96,1536]{1,0:T(8,128)(2,1)S(1)}, u32[]{:S(2)}, u32[]{:S(2)}) collective-permute-start(bf16[96,1536]{1,0:T(8,128)(2,1)S(1)} %get-tuple-element.211), channel_id=1, source_target_pairs={{1,0},{9,8},{17,16},{25,24},{33,32},{41,40},{49,48},{57,56},{65,64... | collective-permute-start | bytes 884744 | tf_op jit(solution)/shard_map/ppermute | solution.py:568
  218.3 7.5 %collective-permute-start.26 = (bf16[96,1536]{1,0:T(8,128)(2,1)S(1)}, bf16[96,1536]{1,0:T(8,128)(2,1)S(1)}, u32[]{:S(2)}, u32[]{:S(2)}) collective-permute-start(bf16[96,1536]{1,0:T(8,128)(2,1)S(1)} %get-tuple-element.215), channel_id=1, source_target_pairs={{1,0},{9,8},{17,16},{25,24},{33,32},{41,40},{49,48},{57,56},{65,64... | collective-permute-start | bytes 884744 | tf_op jit(solution)/shard_map/ppermute | solution.py:568
  242.1 22.0 %collective-permute-start.27 = (bf16[8,2,48,1536]{3,2,1,0:T(8,128)(2,1)S(1)}, bf16[8,2,48,1536]{3,2,1,0:T(8,128)(2,1)S(1)}, u32[]{:S(2)}, u32[]{:S(2)}) collective-permute-start(bf16[8,2,48,1536]{3,2,1,0:T(8,128)(2,1)S(1)} %weight_part.3), channel_id=1, source_target_pairs={{0,8},{8,0},{16,24},{24,16},{32,40},{40,32},{48,56},{56,48},{64,72... | collective-permute-start | bytes 7077896 | tf_op jit(solution)/shard_map/ppermute | solution.py:467
  261.9 2.1 collective-permute-start.28
  264.9 9.2 %collective-permute-start.32 = (bf16[2,56,1536]{2,1,0:T(8,128)(2,1)S(1)}, bf16[2,56,1536]{2,1,0:T(8,128)(2,1)S(1)}, u32[]{:S(2)}, u32[]{:S(2)}) collective-permute-start(bf16[2,56,1536]{2,1,0:T(8,128)(2,1)S(1)} %get-tuple-element.225), channel_id=1, source_target_pairs={{0,128},{8,136},{16,144},{24,152},{32,160},{40,168},{48,176},{56,1... | collective-permute-start | bytes 1032200 | tf_op jit(solution)/shard_map/ppermute | solution.py:470
  265.0 16.5 %collective-permute-start.31 = (bf16[2,56,1536]{2,1,0:T(8,128)(2,1)S(1)}, bf16[2,56,1536]{2,1,0:T(8,128)(2,1)S(1)}, u32[]{:S(2)}, u32[]{:S(2)}) collective-permute-start(bf16[2,56,1536]{2,1,0:T(8,128)(2,1)S(1)} %get-tuple-element.224), channel_id=1, source_target_pairs={{0,128},{8,136},{16,144},{24,152},{32,160},{40,168},{48,176},{56,1... | collective-permute-start | bytes 1032200 | tf_op jit(solution)/shard_map/ppermute | solution.py:470
  274.8 8.1 %collective-permute-start.33 = (bf16[56,1536]{1,0:T(8,128)(2,1)S(1)}, bf16[56,1536]{1,0:T(8,128)(2,1)S(1)}, u32[]{:S(2)}, u32[]{:S(2)}) collective-permute-start(bf16[56,1536]{1,0:T(8,128)(2,1)S(1)} %get-tuple-element.226), channel_id=1, source_target_pairs={{0,16},{8,24},{16,32},{24,40},{32,48},{40,56},{48,64},{56,72},{64,... | collective-permute-start | bytes 516104 | tf_op jit(solution)/shard_map/ppermute | solution.py:464
  276.2 6.7 %collective-permute-start.34 = (bf16[56,1536]{1,0:T(8,128)(2,1)S(1)}, bf16[56,1536]{1,0:T(8,128)(2,1)S(1)}, u32[]{:S(2)}, u32[]{:S(2)}) collective-permute-start(bf16[56,1536]{1,0:T(8,128)(2,1)S(1)} %get-tuple-element.227), channel_id=1, source_target_pairs={{0,112},{8,120},{16,0},{24,8},{32,16},{40,24},{48,32},{56,40},{64,... | collective-permute-start | bytes 516104 | tf_op jit(solution)/shard_map/ppermute | solution.py:464
  280.2 7.8 %collective-permute-start.30 = (bf16[2,56,1536]{2,1,0:T(8,128)(2,1)S(1)}, bf16[2,56,1536]{2,1,0:T(8,128)(2,1)S(1)}, u32[]{:S(2)}, u32[]{:S(2)}) collective-permute-start(bf16[2,56,1536]{2,1,0:T(8,128)(2,1)S(1)} %get-tuple-element.223), channel_id=1, source_target_pairs={{0,128},{8,136},{16,144},{24,152},{32,160},{40,168},{48,176},{56,1... | collective-permute-start | bytes 1032200 | tf_op jit(solution)/shard_map/ppermute | solution.py:470
  283.6 6.7 %collective-permute-start.35 = (bf16[56,1536]{1,0:T(8,128)(2,1)S(1)}, bf16[56,1536]{1,0:T(8,128)(2,1)S(1)}, u32[]{:S(2)}, u32[]{:S(2)}) collective-permute-start(bf16[56,1536]{1,0:T(8,128)(2,1)S(1)} %get-tuple-element.228), channel_id=1, source_target_pairs={{0,16},{8,24},{16,32},{24,40},{32,48},{40,56},{48,64},{56,72},{64,... | collective-permute-start | bytes 516104 | tf_op jit(solution)/shard_map/ppermute | solution.py:464
  283.7 6.6 %collective-permute-start.36 = (bf16[56,1536]{1,0:T(8,128)(2,1)S(1)}, bf16[56,1536]{1,0:T(8,128)(2,1)S(1)}, u32[]{:S(2)}, u32[]{:S(2)}) collective-permute-start(bf16[56,1536]{1,0:T(8,128)(2,1)S(1)} %get-tuple-element.229), channel_id=1, source_target_pairs={{0,112},{8,120},{16,0},{24,8},{32,16},{40,24},{48,32},{56,40},{64,... | collective-permute-start | bytes 516104 | tf_op jit(solution)/shard_map/ppermute | solution.py:464
  287.6 7.4 %collective-permute-start.29 = (bf16[2,56,1536]{2,1,0:T(8,128)(2,1)S(1)}, bf16[2,56,1536]{2,1,0:T(8,128)(2,1)S(1)}, u32[]{:S(2)}, u32[]{:S(2)}) collective-permute-start(bf16[2,56,1536]{2,1,0:T(8,128)(2,1)S(1)} %get-tuple-element.222), channel_id=1, source_target_pairs={{0,128},{8,136},{16,144},{24,152},{32,160},{40,168},{48,176},{56,1... | collective-permute-start | bytes 1032200 | tf_op jit(solution)/shard_map/ppermute | solution.py:470
  291.1 6.6 %collective-permute-start.37 = (bf16[56,1536]{1,0:T(8,128)(2,1)S(1)}, bf16[56,1536]{1,0:T(8,128)(2,1)S(1)}, u32[]{:S(2)}, u32[]{:S(2)}) collective-permute-start(bf16[56,1536]{1,0:T(8,128)(2,1)S(1)} %get-tuple-element.230), channel_id=1, source_target_pairs={{0,16},{8,24},{16,32},{24,40},{32,48},{40,56},{48,64},{56,72},{64,... | collective-permute-start | bytes 516104 | tf_op jit(solution)/shard_map/ppermute | solution.py:464
  292.5 5.2 %collective-permute-start.38 = (bf16[56,1536]{1,0:T(8,128)(2,1)S(1)}, bf16[56,1536]{1,0:T(8,128)(2,1)S(1)}, u32[]{:S(2)}, u32[]{:S(2)}) collective-permute-start(bf16[56,1536]{1,0:T(8,128)(2,1)S(1)} %get-tuple-element.231), channel_id=1, source_target_pairs={{0,112},{8,120},{16,0},{24,8},{32,16},{40,24},{48,32},{56,40},{64,... | collective-permute-start | bytes 516104 | tf_op jit(solution)/shard_map/ppermute | solution.py:464
  298.4 6.6 %collective-permute-start.39 = (bf16[56,1536]{1,0:T(8,128)(2,1)S(1)}, bf16[56,1536]{1,0:T(8,128)(2,1)S(1)}, u32[]{:S(2)}, u32[]{:S(2)}) collective-permute-start(bf16[56,1536]{1,0:T(8,128)(2,1)S(1)} %get-tuple-element.233), channel_id=1, source_target_pairs={{0,16},{8,24},{16,32},{24,40},{32,48},{40,56},{48,64},{56,72},{64,... | collective-permute-start | bytes 516104 | tf_op jit(solution)/shard_map/ppermute | solution.py:464
  305.1 4.6 %collective-permute-start.44 = (bf16[56,1536]{1,0:T(8,128)(2,1)S(1)}, bf16[56,1536]{1,0:T(8,128)(2,1)S(1)}, u32[]{:S(2)}, u32[]{:S(2)}) collective-permute-start(bf16[56,1536]{1,0:T(8,128)(2,1)S(1)} %get-tuple-element.240), channel_id=1, source_target_pairs={{0,112},{8,120},{16,0},{24,8},{32,16},{40,24},{48,32},{56,40},{64,... | collective-permute-start | bytes 516104 | tf_op jit(solution)/shard_map/ppermute | solution.py:464
  306.9 5.5 %collective-permute-start.40 = (bf16[56,1536]{1,0:T(8,128)(2,1)S(1)}, bf16[56,1536]{1,0:T(8,128)(2,1)S(1)}, u32[]{:S(2)}, u32[]{:S(2)}) collective-permute-start(bf16[56,1536]{1,0:T(8,128)(2,1)S(1)} %get-tuple-element.240), channel_id=1, source_target_pairs={{0,16},{8,24},{16,32},{24,40},{32,48},{40,56},{48,64},{56,72},{64,... | collective-permute-start | bytes 516104 | tf_op jit(solution)/shard_map/ppermute | solution.py:464
  312.4 13.6 %collective-permute-start.50 = (bf16[3,56,1536]{2,1,0:T(8,128)(2,1)S(1)}, bf16[3,56,1536]{2,1,0:T(8,128)(2,1)S(1)}, u32[]{:S(2)}, u32[]{:S(2)}) collective-permute-start(bf16[3,56,1536]{2,1,0:T(8,128)(2,1)S(1)} %pad_maximum_fusion.1.rest_0_), channel_id=1, source_target_pairs={{0,128},{8,136},{16,144},{24,152},{32,160},{40,168},{48,176},{56,1... | collective-permute-start | bytes 1548296 | tf_op jit(solution)/shard_map/ppermute | solution.py:470
  312.8 4.6 %collective-permute-start.45 = (bf16[56,1536]{1,0:T(8,128)(2,1)S(1)}, bf16[56,1536]{1,0:T(8,128)(2,1)S(1)}, u32[]{:S(2)}, u32[]{:S(2)}) collective-permute-start(bf16[56,1536]{1,0:T(8,128)(2,1)S(1)} %collective-permute-done.44), channel_id=1, source_target_pairs={{0,112},{8,120},{16,0},{24,8},{32,16},{40,24},{48,32},{56,40},{64,... | collective-permute-start | bytes 516104 | tf_op jit(solution)/shard_map/ppermute | solution.py:464
  312.8 5.9 %collective-permute-start.41 = (bf16[56,1536]{1,0:T(8,128)(2,1)S(1)}, bf16[56,1536]{1,0:T(8,128)(2,1)S(1)}, u32[]{:S(2)}, u32[]{:S(2)}) collective-permute-start(bf16[56,1536]{1,0:T(8,128)(2,1)S(1)} %collective-permute-done.40), channel_id=1, source_target_pairs={{0,16},{8,24},{16,32},{24,40},{32,48},{40,56},{48,64},{56,72},{64,... | collective-permute-start | bytes 516104 | tf_op jit(solution)/shard_map/ppermute | solution.py:464
  318.7 10.2 %collective-permute-start.51 = (bf16[2,56,1536]{2,1,0:T(8,128)(2,1)S(1)}, bf16[2,56,1536]{2,1,0:T(8,128)(2,1)S(1)}, u32[]{:S(2)}, u32[]{:S(2)}) collective-permute-start(bf16[2,56,1536]{2,1,0:T(8,128)(2,1)S(1)} %pad_maximum_fusion.3.rest_2_), channel_id=1, source_target_pairs={{0,128},{8,136},{16,144},{24,152},{32,160},{40,168},{48,176},{56,1... | collective-permute-start | bytes 1032200 | tf_op jit(solution)/shard_map/ppermute | solution.py:470
  319.5 6.4 %collective-permute-start.46 = (bf16[56,1536]{1,0:T(8,128)(2,1)S(1)}, bf16[56,1536]{1,0:T(8,128)(2,1)S(1)}, u32[]{:S(2)}, u32[]{:S(2)}) collective-permute-start(bf16[56,1536]{1,0:T(8,128)(2,1)S(1)} %collective-permute-done.45), channel_id=1, source_target_pairs={{0,112},{8,120},{16,0},{24,8},{32,16},{40,24},{48,32},{56,40},{64,... | collective-permute-start | bytes 516104 | tf_op jit(solution)/shard_map/ppermute | solution.py:464
  319.5 6.4 %collective-permute-start.42 = (bf16[56,1536]{1,0:T(8,128)(2,1)S(1)}, bf16[56,1536]{1,0:T(8,128)(2,1)S(1)}, u32[]{:S(2)}, u32[]{:S(2)}) collective-permute-start(bf16[56,1536]{1,0:T(8,128)(2,1)S(1)} %collective-permute-done.41), channel_id=1, source_target_pairs={{0,16},{8,24},{16,32},{24,40},{32,48},{40,56},{48,64},{56,72},{64,... | collective-permute-start | bytes 516104 | tf_op jit(solution)/shard_map/ppermute | solution.py:464
  328.9 22.6 %collective-permute-start.52 = (bf16[12,56,1536]{2,1,0:T(8,128)(2,1)S(1)}, bf16[12,56,1536]{2,1,0:T(8,128)(2,1)S(1)}, u32[]{:S(2)}, u32[]{:S(2)}) collective-permute-start(bf16[12,56,1536]{2,1,0:T(8,128)(2,1)S(1)} %constant_dynamic-update-slice_fusion), channel_id=1, source_target_pairs={{0,8},{8,0},{16,24},{24,16},{32,40},{40,32},{48,56},{56,48},{64,72... | collective-permute-start | bytes 6193160 | tf_op jit(solution)/shard_map/ppermute | solution.py:467
  337.0 7.1 %collective-permute-start.43 = (bf16[56,1536]{1,0:T(8,128)(2,1)S(1)}, bf16[56,1536]{1,0:T(8,128)(2,1)S(1)}, u32[]{:S(2)}, u32[]{:S(2)}) collective-permute-start(bf16[56,1536]{1,0:T(8,128)(2,1)S(1)} %collective-permute-done.42), channel_id=1, source_target_pairs={{0,16},{8,24},{16,32},{24,40},{32,48},{40,56},{48,64},{56,72},{64,... | collective-permute-start | bytes 516104 | tf_op jit(solution)/shard_map/ppermute | solution.py:464
  337.0 12.9 %collective-permute-start.47 = (bf16[2,56,1536]{2,1,0:T(8,128)(2,1)S(1)}, bf16[2,56,1536]{2,1,0:T(8,128)(2,1)S(1)}, u32[]{:S(2)}, u32[]{:S(2)}) collective-permute-start(bf16[2,56,1536]{2,1,0:T(8,128)(2,1)S(1)} %pad_maximum_fusion.2.rest_3_), channel_id=1, source_target_pairs={{0,128},{8,136},{16,144},{24,152},{32,160},{40,168},{48,176},{56,1... | collective-permute-start | bytes 1032200 | tf_op jit(solution)/shard_map/ppermute | solution.py:470
  344.1 5.8 %collective-permute-start.48 = (bf16[1,56,1536]{2,1,0:T(8,128)(2,1)S(1)}, bf16[1,56,1536]{2,1,0:T(8,128)(2,1)S(1)}, u32[]{:S(2)}, u32[]{:S(2)}) collective-permute-start(bf16[1,56,1536]{2,1,0:T(8,128)(2,1)S(1)} %bitcast.96), channel_id=1, source_target_pairs={{0,128},{8,136},{16,144},{24,152},{32,160},{40,168},{48,176},{56,1... | collective-permute-start | bytes 516104 | tf_op jit(solution)/shard_map/ppermute | solution.py:470
  350.0 4.0 %collective-permute-start.49 = (bf16[4,56,1536]{2,1,0:T(8,128)(2,1)S(1)}, bf16[4,56,1536]{2,1,0:T(8,128)(2,1)S(1)}, u32[]{:S(2)}, u32[]{:S(2)}) collective-permute-start(bf16[4,56,1536]{2,1,0:T(8,128)(2,1)S(1)} %pad_maximum_fusion), channel_id=1, source_target_pairs={{0,8},{8,0},{16,24},{24,16},{32,40},{40,32},{48,56},{56,48},{64,72... | collective-permute-start | bytes 2064392 | tf_op jit(solution)/shard_map/ppermute | solution.py:467
